TPU v7x, 32 devices: a whole 2x2x4 slice. The times are simulated.
32 devices in a mesh: dp: 8 (over z, y), tensor: 4 (over x, core).
Axes of the slice: x: 2, y: 2, z: 4, core: 2. Of those that a mesh axis runs over, the one named last changes fastest.
Arguments:
- gene_ids: int32 [16384], P('dp'), may hold values from 0 to 35999
- know_ids: int32 [5, 16384], P(None, 'dp'), may hold values from 0 to 1023
- lengths: int32 [8], P('dp'), may hold values from 1 to 2048, as said below
- tables: bfloat16 [41120, 768], P('dp', 'tensor'), may hold values from -6 to 6
- norm_gain: bfloat16 [2, 768], replicated, may hold values from 0.5 to 1.5
- norm_bias: bfloat16 [2, 768], replicated, may hold values from -4 to 4
- qkv_weight: bfloat16 [3, 768, 768], P(None, None, 'tensor'), may hold values from -0.21875 to 0.21875
- qv_bias: bfloat16 [2, 768], P(None, 'tensor'), may hold values from -0.75 to 0.75
- out_weight: bfloat16 [768, 768], P('tensor'), may hold values from -1.75 to 1.75
- out_bias: bfloat16 [768], replicated, may hold values from -4 to 4
- up_weight: bfloat16 [768, 3072], P(None, 'tensor'), may hold values from -0.21875 to 0.21875
- up_bias: bfloat16 [3072], P('tensor'), may hold values from -6 to 6
- down_weight: bfloat16 [3072, 768], P('tensor'), may hold values from -0.109375 to 0.109375
- down_bias: bfloat16 [768], replicated, may hold values from -4 to 4
- cotangent: bfloat16 [16384, 768], P('dp'), may hold values from -6 to 6
Outputs:
- out: bfloat16 [16384, 768], P('dp')
- input_grad: float32 [16384, 768], P('dp')
- tables_grad: float32 [41120, 768], P('dp', 'tensor')
- norm_gain_grad: float32 [2, 768], replicated
- norm_bias_grad: float32 [2, 768], replicated
- qkv_grad: float32 [3, 768, 768], P(None, None, 'tensor')
- qv_bias_grad: float32 [2, 768], P(None, 'tensor')
- out_weight_grad: float32 [768, 768], P('tensor')
- out_bias_grad: float32 [768], replicated
- up_weight_grad: float32 [768, 3072], P(None, 'tensor')
- up_bias_grad: float32 [3072], P('tensor')
- down_weight_grad: float32 [3072, 768], P('tensor')
- down_bias_grad: float32 [768], replicated
Inputs may be any that keep to these rules, and one draw needn't show every extreme that they name: `lengths`: every cell has at least one gene, and some cell has exactly 2048.
All inputs are finite; a program needn't handle non-finite values.
Results may differ from a plain program's by a relative error of at most 0.012.
The roundings to bfloat16 on the way count: a program that leaves them out, or rounds other values in their place, can miss the bound.
Values may be sent and summed in bfloat16 or wider, within the bound.
No kernel may reach another device: no remote copies, remote signals or barrier semaphores. Data moves between devices by JAX's collectives and lax.ppermute only.
A program may use at most 256 MiB of HBM per device.

v0:
```python
from functools import partial

import jax
import jax.numpy as jnp
from jax import lax
from jax.experimental import pallas as pl
from jax.experimental.pallas import tpu as pltpu
from jax.sharding import PartitionSpec as P

HEADS = 12
VOCAB = 36000
KNOW = 1024
TABLES = 5
SHARDS = 8
norm_eps = 1e-05
BF = jnp.bfloat16
F32 = jnp.float32
I32 = jnp.int32
BIG = 56 * 1024 * 1024


def params():
    return pltpu.CompilerParams(vmem_limit_bytes=BIG)


def cost(micros):
    return pl.CostEstimate(
        flops=int(micros * 9e8), bytes_accessed=int(micros * 3e6), transcendentals=0
    )


def shape(dims, kind):
    return jax.ShapeDtypeStruct(dims, kind)


def dot_nt(left, right):
    return lax.dot_general(left, right, (((1,), (1,)), ((), ())), preferred_element_type=F32)


def dot_tn(left, right):
    return lax.dot_general(left, right, (((0,), (0,)), ((), ())), preferred_element_type=F32)


def dot_nn(left, right):
    return jnp.dot(left, right, preferred_element_type=F32)


def whole(dims):
    return pl.BlockSpec(dims, lambda i, *s: (0,) * len(dims))


def hot(condition):
    return condition.astype(F32).astype(BF)


def rows_like(dims):
    return lax.broadcasted_iota(I32, dims, 0)


def lanes_like(dims):
    return lax.broadcasted_iota(I32, dims, 1)


def after(value, *others):
    return lax.optimization_barrier((value, others))[0]


def hop(value, axis, flip):
    count = lax.axis_size(axis)
    return lax.ppermute(value, axis, [(i, i ^ flip) for i in range(count)])


def gather_four(block):
    far = hop(block, "tensor", 2)
    return [block, hop(block, "tensor", 1), far, hop(far, "tensor", 1)]


def swap_four(pieces):
    return [pieces[0]] + [hop(pieces[j], "tensor", j) for j in (1, 2, 3)]


def route_kernel(where_ref, ids_ref, lists_ref, slot_ref, most_ref, *, owned, slots):
    group, turn = where_ref[0], where_ref[1]
    ids = ids_ref[...]
    groups, count = ids.shape
    wanted = (ids >= group * owned) & (ids < (group + 1) * owned)
    mine = jnp.broadcast_to(ids[0:1, :], (groups, count))
    owners = rows_like((groups, count))
    held = (mine >= owners * owned) & (mine < (owners + 1) * owned)
    flags = jnp.concatenate([wanted.astype(F32), held.astype(F32)], 0)
    sums = flags
    lanes = lanes_like(flags.shape)
    step = 1
    while step < count:
        sums = sums + jnp.where(lanes >= step, pltpu.roll(sums, step, 1), 0.0)
        step *= 2
    low = (turn * slots).astype(F32)
    ranks = sums[:groups] - 1.0 - low
    ranks = jnp.where(wanted & (ranks >= 0.0) & (ranks < slots), ranks, -1.0).astype(I32)
    plus = jnp.where(wanted, ids - group * owned + 1, 0)
    spots = rows_like((slots, count))
    halves = rows_like((16, count))
    for k in range(groups):
        number = jnp.broadcast_to(plus[k : k + 1, :], (16, count))
        parts = jnp.where(halves == 0, number >> 8, jnp.where(halves == 1, number & 255, 0))
        parts = parts.astype(F32).astype(BF)
        match = hot(spots == ranks[k : k + 1, :])
        found = dot_nt(parts, match)
        lists_ref[group ^ k] = (found[0:1, :] * 256.0 + found[1:2, :]).astype(I32) - 1
    own = sums[groups:] - 1.0 - low
    good = held & (own >= 0.0) & (own < slots)
    slot = jnp.where(good, owners.astype(F32) * slots + own + 1.0, 0.0)
    slot = jnp.sum(slot, 0, keepdims=True) - 1.0
    slot_ref[...] = slot.astype(I32)
    most = jnp.zeros((groups, 1), F32)
    for o in range(groups):
        here = (ids >= o * owned) & (ids < (o + 1) * owned)
        most = jnp.maximum(most, jnp.sum(here.astype(F32), 1, keepdims=True))
    most_ref[...] = jnp.broadcast_to(jnp.max(most, 0, keepdims=True), (8, 128)).astype(I32)


def route(group, turn, ids, owned, slots):
    groups, count = ids.shape

    return pl.pallas_call(
        partial(route_kernel, owned=owned, slots=slots),
        grid_spec=pltpu.PrefetchScalarGridSpec(
            num_scalar_prefetch=1,
            grid=(1,),
            in_specs=[whole(ids.shape)],
            out_specs=[
                whole((groups, 1, slots)),
                whole((1, count)),
                whole((8, 128)),
            ],
        ),
        out_shape=[
            shape((groups, 1, slots), I32),
            shape((1, count), I32),
            shape((8, 128), I32),
        ],
        compiler_params=params(),
        cost_estimate=cost(8),
        name="route",
    )(jnp.stack([group, turn]), ids)


def pick_kernel(list_ref, table_ref, out_ref, *, chunk):
    wanted = list_ref[0]
    size = table_ref.shape[1]
    total = jnp.zeros(out_ref.shape[1:], F32)
    for start in range(0, size, chunk):
        part = min(chunk, size - start)
        match = hot(rows_like((part, wanted.shape[1])) == wanted - start)
        total += dot_nn(table_ref[:, start : start + part], match)
    out_ref[0] = total.astype(BF)


def pick(lists, table):
    groups, _, slots = lists.shape
    columns = table.shape[0]
    return pl.pallas_call(
        partial(pick_kernel, chunk=512),
        grid=(groups,),
        in_specs=[
            pl.BlockSpec((1, 1, slots), lambda i: (i, 0, 0)),
            pl.BlockSpec(table.shape, lambda i: (0, 0)),
        ],
        out_specs=pl.BlockSpec((1, columns, slots), lambda i: (i, 0, 0)),
        out_shape=shape((groups, columns, slots), BF),
        compiler_params=params(),
        cost_estimate=cost(12),
        name="pick",
    )(lists, table)


def embed_kernel(
    where_ref, slot_ref, code_ref, moved_ref, know_ref, extra_ref, out_ref, table_ref, *, order
):
    groups, columns, slots = moved_ref.shape
    shards, _, size = know_ref.shape

    @pl.when(pl.program_id(0) == 0)
    def _():
        for k in range(shards):
            at = pl.multiple_of((where_ref[0] ^ order[k]) * size, 128)
            table_ref[:, pl.ds(at, size)] = know_ref[k]

    slot = slot_ref[...]
    block = slot.shape[1]
    total = extra_ref[...].astype(F32)
    for n in range(groups):
        match = hot(rows_like((slots, block)) == slot - n * slots)
        total += dot_nn(moved_ref[n], match)
    for j in range(TABLES):
        match = hot(rows_like((KNOW, block)) == code_ref[j : j + 1, :])
        total += dot_nn(table_ref[:, j * KNOW : (j + 1) * KNOW], match)
    out_ref[...] = total.astype(BF)


def embed(half, turned, order, slot, codes, moved, know, extra):
    count = slot.shape[1] // 2
    columns = moved.shape[1]
    block = min(512, count)
    steps = count // block
    return pl.pallas_call(
        partial(embed_kernel, order=order),
        grid_spec=pltpu.PrefetchScalarGridSpec(
            num_scalar_prefetch=1,
            grid=(steps,),
            in_specs=[
                pl.BlockSpec((1, block), lambda i, s: (0, steps * half + i)),
                pl.BlockSpec((TABLES, block), lambda i, s: (0, steps * half + i)),
                whole(moved.shape),
                whole(know.shape),
                pl.BlockSpec((columns, block), lambda i, s: (0, steps * half + i)),
            ],
            out_specs=pl.BlockSpec((columns, block), lambda i, s: (0, i)),
            scratch_shapes=[pltpu.VMEM((columns, TABLES * KNOW), BF)],
        ),
        out_shape=shape((columns, count), BF),
        compiler_params=params(),
        cost_estimate=cost(6),
        name="embed",
    )(turned[None], slot, codes, moved, know, extra)


def more_kernel(slot_ref, moved_ref, have_ref, out_ref):
    groups, columns, slots = moved_ref.shape
    slot = slot_ref[...]
    block = slot.shape[1]
    total = have_ref[...].astype(F32)
    for n in range(groups):
        match = hot(rows_like((slots, block)) == slot - n * slots)
        total += dot_nn(moved_ref[n], match)
    out_ref[...] = total.astype(BF)


def embed_more(slot, moved, have):
    columns, count = have.shape
    block = min(512, count)
    return pl.pallas_call(
        more_kernel,
        grid=(count // block,),
        in_specs=[
            pl.BlockSpec((1, block), lambda i: (0, i)),
            pl.BlockSpec(moved.shape, lambda i: (0, 0, 0)),
            pl.BlockSpec((columns, block), lambda i: (0, i)),
        ],
        out_specs=pl.BlockSpec((columns, block), lambda i: (0, i)),
        out_shape=shape((columns, count), BF),
        compiler_params=params(),
        name="embed_more",
    )(slot, moved, have)


def bucket_kernel(slot_ref, near_ref, far_ref, out_ref):
    slots = out_ref.shape[2]
    half = near_ref.shape[1]
    start = pl.program_id(0) * slots
    match = hot(rows_like((slots, 2 * half)) == slot_ref[...] - start)
    total = dot_nt(near_ref[...], match[:, :half]) + dot_nt(far_ref[...], match[:, half:])
    out_ref[0] = total.astype(BF)


def bucket(slot, near, far, groups, slots):
    columns = near.shape[0]
    return pl.pallas_call(
        bucket_kernel,
        grid=(groups,),
        in_specs=[whole(slot.shape), whole(near.shape), whole(far.shape)],
        out_specs=pl.BlockSpec((1, columns, slots), lambda i: (i, 0, 0)),
        out_shape=shape((groups, columns, slots), BF),
        compiler_params=params(),
        cost_estimate=cost(0.2),
        name="bucket",
    )(slot, near, far)


def know_grad_kernel(where_ref, code_ref, *refs, base, parts):
    out_ref = refs[-1]
    size = out_ref.shape[2]
    count = code_ref.shape[1]
    step = pl.program_id(0)
    start = (where_ref[0] ^ (base + 4 * (step % 2) + step // 2)) * size
    first = start // KNOW
    last = (start + size - 1) // KNOW
    rows = rows_like((size, count)) + start
    match = rows == code_ref[pl.ds(first, 1), :] + first * KNOW
    match = match | (rows == code_ref[pl.ds(last, 1), :] + last * KNOW)
    match = hot(match)
    width = count // parts
    total = sum(dot_nt(refs[k][...], match[:, k * width : (k + 1) * width]) for k in range(parts))
    if len(refs) > parts + 1:
        total += refs[parts][0].astype(F32)
    out_ref[0] = total.astype(BF)


def know_grads(turned, codes, start, data, base, have):
    columns, count = data[0].shape
    size = TABLES * KNOW // SHARDS
    part = pl.BlockSpec((1, columns, size), lambda i, s: (i, 0, 0))
    return pl.pallas_call(
        partial(know_grad_kernel, base=base, parts=len(data)),
        grid_spec=pltpu.PrefetchScalarGridSpec(
            num_scalar_prefetch=1,
            grid=(4,),
            in_specs=[pl.BlockSpec((TABLES, count * len(data)), lambda i, s: (0, start))]
            + [whole(d.shape) for d in data]
            + [part] * len(have),
            out_specs=part,
        ),
        out_shape=shape((4, columns, size), BF),
        compiler_params=params(),
        cost_estimate=cost(0.2),
        name="know_grads",
    )(turned[None], codes, *data, *have)


def collect_kernel(list_ref, sent_ref, out_ref):
    groups, columns, slots = sent_ref.shape
    block = out_ref.shape[1]
    start = pl.program_id(0) * block
    total = jnp.zeros((columns, block), F32)
    for n in range(groups):
        match = hot(lanes_like((slots, block)) == list_ref[n] - start)
        total += dot_nn(sent_ref[n], match)
    out_ref[...] = total


def collect(lists, sent, owned):
    groups, columns, slots = sent.shape
    block = 512
    return pl.pallas_call(
        collect_kernel,
        grid=(pl.cdiv(owned, block),),
        in_specs=[
            pl.BlockSpec(lists.shape, lambda i: (0, 0, 0)),
            pl.BlockSpec(sent.shape, lambda i: (0, 0, 0)),
        ],
        out_specs=pl.BlockSpec((columns, block), lambda i: (0, i)),
        out_shape=shape((columns, owned), F32),
        compiler_params=params(),
        cost_estimate=cost(15),
        name="collect",
    )(lists, sent)


def add_know_kernel(where_ref, have_ref, *refs, order, window):
    know_refs, out_ref, table_ref = refs[:-2], refs[-2], refs[-1]
    columns, size = know_refs[0].shape
    step = pl.program_id(0)

    @pl.when(step == 0)
    def _():
        for k, know_ref in enumerate(know_refs):
            table_ref[:, order[k] * size : (order[k] + 1) * size] = know_ref[...]

    block = out_ref.shape[1]
    total = len(know_refs) * size
    origin = step * block - where_ref[0]
    base = jnp.clip((origin // 128) * 128, 0, total - window)
    base = pl.multiple_of(base, 128)
    part = table_ref[:, pl.ds(base, window)].astype(F32)
    turn = lax.rem(lax.rem(base - origin, window) + window, window)
    part = pltpu.roll(part, turn, 1)[:, :block]
    index = lanes_like((columns, block)) + origin
    out_ref[...] = have_ref[...] + jnp.where((index >= 0) & (index < total), part, 0.0)


def add_know(offset, have, know, order):
    columns, owned = have.shape
    block = 1024
    part = pl.BlockSpec((columns, block), lambda i, s: (0, i))
    return pl.pallas_call(
        partial(add_know_kernel, order=order, window=block + 128),
        grid_spec=pltpu.PrefetchScalarGridSpec(
            num_scalar_prefetch=1,
            grid=(pl.cdiv(owned, block),),
            in_specs=[part] + [pl.BlockSpec(k.shape, lambda i, s: (0, 0)) for k in know],
            out_specs=part,
            scratch_shapes=[pltpu.VMEM((columns, TABLES * KNOW), BF)],
        ),
        out_shape=shape((columns, owned), F32),
        input_output_aliases={1: 0},
        compiler_params=params(),
        cost_estimate=cost(0.2),
        name="add_know",
    )(offset[None], have, *know)


def collect_more_kernel(list_ref, sent_ref, have_ref, out_ref):
    groups, columns, slots = sent_ref.shape
    block = out_ref.shape[1]
    start = pl.program_id(0) * block
    total = have_ref[...]
    for n in range(groups):
        match = hot(lanes_like((slots, block)) == list_ref[n] - start)
        total += dot_nn(sent_ref[n], match)
    out_ref[...] = total


def collect_more(lists, sent, have):
    columns, owned = have.shape
    block = 512
    return pl.pallas_call(
        collect_more_kernel,
        grid=(pl.cdiv(owned, block),),
        in_specs=[
            pl.BlockSpec(lists.shape, lambda i: (0, 0, 0)),
            pl.BlockSpec(sent.shape, lambda i: (0, 0, 0)),
            pl.BlockSpec((columns, block), lambda i: (0, i)),
        ],
        out_specs=pl.BlockSpec((columns, block), lambda i: (0, i)),
        out_shape=shape((columns, owned), F32),
        compiler_params=params(),
        name="collect_more",
    )(lists, sent, have)


def project_kernel(where_ref, e0, e1, e2, e3, vec_ref, w_ref, bias_ref, f_ref, p_ref, col_ref):
    col_ref[...] = vec_ref[...].T
    pieces = [e[...].astype(F32) for e in (e0, e1, e2, e3)]
    part = pieces[0].shape[0]
    width = 4 * part
    average = sum(jnp.sum(p, 0, keepdims=True) for p in pieces) / width
    pieces = [p - average for p in pieces]
    spread = sum(jnp.sum(p * p, 0, keepdims=True) for p in pieces) / width
    scale = lax.rsqrt(spread + norm_eps)
    for j in range(4):
        rows = pl.ds(pl.multiple_of((where_ref[0] ^ j) * part, 64), part)
        unit = pieces[j] * scale
        f_ref[rows, :] = (unit * col_ref[rows, 0:1] + col_ref[rows, 1:2]).astype(BF)
    p_ref[...] = (dot_nn(w_ref[...], f_ref[...]) + bias_ref[...].T[:, 0:1]).astype(BF)


def project(place, pieces, vectors, weight, bias):
    part, count = pieces[0].shape
    block = count // 2

    def piece_spec(j):
        return pl.BlockSpec((part, block), lambda i, s: (0, i ^ (j & 1)))

    return pl.pallas_call(
        project_kernel,
        grid_spec=pltpu.PrefetchScalarGridSpec(
            num_scalar_prefetch=1,
            grid=(2,),
            in_specs=[piece_spec(j) for j in range(4)]
            + [whole(vectors.shape), whole(weight.shape), whole(bias.shape)],
            scratch_shapes=[pltpu.VMEM((4 * part, 8), F32)],
            out_specs=[
                pl.BlockSpec((4 * part, block), lambda i, s: (0, i)),
                pl.BlockSpec((weight.shape[0], block), lambda i, s: (0, i)),
            ],
        ),
        out_shape=[shape((4 * part, count), BF), shape((weight.shape[0], count), BF)],
        compiler_params=params(),
        cost_estimate=cost(4),
        name="project",
    )(place[None], *pieces, vectors, weight, bias)


def two_parts(value):
    high = value.astype(BF).astype(F32)
    return high, value - high


def widened(part, head, head_dim, extra):
    columns, count = part.shape
    rows = rows_like((columns, count))
    keep = (rows >= head * head_dim) & (rows < (head + 1) * head_dim)
    kept = jnp.where(keep, part, 0.0)
    below = rows_like((256 - columns, count))
    rest = jnp.zeros((256 - columns, count), F32)
    for at, row in enumerate(extra):
        rest = jnp.where(below == at, row, rest)
    return jnp.concatenate([kept, rest], 0).astype(BF)


def attend_kernel(
    q_ref, near_ref, far_ref, mask_ref, out_ref, lse_ref, keys_ref, values_ref, *, heads, head_dim
):
    columns = heads * head_dim
    half = near_ref.shape[1]
    count = 2 * half

    @pl.when(pl.program_id(0) == 0)
    def _():
        rest = rows_like((256 - columns, count))
        rest = jnp.where(rest == 0, mask_ref[...], 0.0)
        for at, ref in ((0, near_ref), (half, far_ref)):
            k = ref[columns : 2 * columns, :].astype(F32)
            k = jnp.concatenate([k, rest[:, at : at + half]], 0)
            keys_ref[at : at + half, :] = k.T.astype(BF)
            values_ref[:, at : at + half] = ref[2 * columns :, :]

    queries = q_ref[...].astype(F32) * head_dim ** (-0.5)
    ones = jnp.ones((1, queries.shape[1]), F32)
    for h in range(heads):
        scores = dot_nn(keys_ref[...], widened(queries, h, head_dim, [ones]))
        highest = jnp.max(scores, 0, keepdims=True)
        expanded = jnp.exp(scores - highest)
        total = jnp.sum(expanded, 0, keepdims=True)
        rows = slice(h * head_dim, (h + 1) * head_dim)
        out_ref[rows, :] = (dot_nn(values_ref[rows, :], expanded.astype(BF)) / total).astype(BF)
        lse_ref[h : h + 1, :] = highest + jnp.log(total)


def attend(near, far, mask, half, heads, head_dim):
    count = near.shape[1]
    columns = heads * head_dim
    block = 256
    return pl.pallas_call(
        partial(attend_kernel, heads=heads, head_dim=head_dim),
        grid=(count // block,),
        in_specs=[
            pl.BlockSpec((columns, block), lambda i: (0, i)),
            whole(near.shape),
            whole(far.shape),
            whole(mask.shape),
        ],
        out_specs=[
            pl.BlockSpec((columns, block), lambda i: (0, i)),
            pl.BlockSpec((8, block), lambda i: (0, i)),
        ],
        out_shape=[shape((columns, count), BF), shape((8, count), F32)],
        scratch_shapes=[pltpu.VMEM((2 * count, 256), BF), pltpu.VMEM((columns, 2 * count), BF)],
        compiler_params=params(),
        cost_estimate=cost(16),
        name="attend",
    )((near, far)[half], near, far, mask)


def attend_back_kernel(
    near_ref, far_ref, mask_ref, o_near, o_far, g_ref, lse_near, lse_far, d_ref,
    keys_ref, values_ref, flat_ref, q_ref, o_ref, lse_ref, dk_acc, dv_acc, *, heads, head_dim,
):
    step = pl.program_id(0)
    columns = heads * head_dim
    half = near_ref.shape[1]
    count = 2 * half
    block = g_ref.shape[1]
    steps = half // block

    @pl.when(step < steps)
    def _():
        at = pl.ds(pl.multiple_of(step * block, 128), block)
        q_ref[...] = near_ref[:columns, at]
        o_ref[...] = o_near[:, at]
        lse_ref[...] = lse_near[:, at]

    @pl.when(step >= steps)
    def _():
        at = pl.ds(pl.multiple_of((step - steps) * block, 128), block)
        q_ref[...] = far_ref[:columns, at]
        o_ref[...] = o_far[:, at]
        lse_ref[...] = lse_far[:, at]

    @pl.when(step == 0)
    def _():
        rest = rows_like((256 - columns, count))
        ones = jnp.where((rest == 1) | (rest == 2), 1.0, 0.0)
        with_mask = jnp.where(rest == 0, mask_ref[...], ones)
        for at, ref in ((0, near_ref), (half, far_ref)):
            part = slice(at, at + half)
            k = ref[columns : 2 * columns, :]
            v = ref[2 * columns :, :].astype(F32)
            flat_ref[:, part] = k
            k = jnp.concatenate([k.astype(F32), with_mask[:, part]], 0)
            keys_ref[part, :] = k.T.astype(BF)
            values_ref[part, :] = jnp.concatenate([v, ones[:, part]], 0).T.astype(BF)
        dk_acc[...] = jnp.zeros_like(dk_acc)
        dv_acc[...] = jnp.zeros_like(dv_acc)

    score_scale = head_dim ** (-0.5)
    queries = q_ref[...].astype(F32) * score_scale
    grads = g_ref[...].astype(F32)
    inner = grads * o_ref[...].astype(F32)
    by_query = queries.T
    by_grad = grads.T
    lanes = lanes_like(by_query.shape)
    one = jnp.ones((1, block), F32)
    zero = jnp.zeros((1, block), F32)
    here = pl.ds(pl.multiple_of(step * block, 128), block)
    for h in range(heads):
        rows = slice(h * head_dim, (h + 1) * head_dim)
        keep = (lanes >= h * head_dim) & (lanes < (h + 1) * head_dim)
        lse = two_parts(-lse_ref[h : h + 1, :])
        delta = two_parts(-jnp.sum(inner[rows, :], 0, keepdims=True))
        scores = dot_nn(keys_ref[...], widened(queries, h, head_dim, [one, *lse]))
        probs = jnp.exp(scores)
        dv_acc[...] += dot_nn(probs.astype(BF), jnp.where(keep, by_grad, 0.0).astype(BF))
        grad_probs = dot_nn(values_ref[...], widened(grads, h, head_dim, [zero, *delta]))
        grad_scores = (probs * grad_probs).astype(BF)
        dk_acc[...] += dot_nn(grad_scores, jnp.where(keep, by_query, 0.0).astype(BF))
        d_ref[rows, here] = (dot_nn(flat_ref[rows, :], grad_scores) * score_scale).astype(BF)

    @pl.when(step == pl.num_programs(0) - 1)
    def _():
        d_ref[columns : 2 * columns, :] = dk_acc[...].T.astype(BF)
        d_ref[2 * columns :, :] = dv_acc[...].T.astype(BF)


def attend_back(near, far, mask, out, grad, lse, heads, head_dim):
    rows, half = near.shape
    count = 2 * half
    columns = heads * head_dim
    block = 256
    arrays = (near, far, mask, *out, grad, *lse)
    specs = [whole(a.shape) for a in arrays]
    specs[5] = pl.BlockSpec((columns, block), lambda i: (0, i))
    return pl.pallas_call(
        partial(attend_back_kernel, heads=heads, head_dim=head_dim),
        grid=(count // block,),
        in_specs=specs,
        out_specs=whole((rows, count)),
        out_shape=shape((rows, count), BF),
        scratch_shapes=[
            pltpu.VMEM((count, 256), BF),
            pltpu.VMEM((count, 256), BF),
            pltpu.VMEM((columns, count), BF),
            pltpu.VMEM((columns, block), BF),
            pltpu.VMEM((columns, block), BF),
            pltpu.VMEM((8, block), F32),
            pltpu.VMEM((count, columns), F32),
            pltpu.VMEM((count, columns), F32),
        ],
        compiler_params=params(),
        cost_estimate=cost(38),
        name="attend_back",
    )(*arrays)


def to_second_kernel(where_ref, *refs):
    h_refs, e_refs, o_refs = refs[0:4], refs[4:8], refs[8:12]
    vec_ref, resid_ref, upper_ref, lower_ref, emb_ref = refs[12:]
    part = h_refs[0].shape[0]
    for j in range(4):
        rows = pl.ds(pl.multiple_of((where_ref[0] ^ j) * part, 64), part)
        emb_ref[rows, :] = e_refs[j][...].astype(F32)
    resid = emb_ref[...].T + vec_ref[0:1, :]
    for j in range(4):
        resid += dot_tn(h_refs[j][...], o_refs[j][...])
    resid_ref[...] = resid
    centered = resid - jnp.mean(resid, -1, keepdims=True)
    spread = jnp.mean(centered * centered, -1, keepdims=True)
    unit = centered * lax.rsqrt(spread + norm_eps)
    second = (unit * vec_ref[1:2, :] + vec_ref[2:3, :]).astype(BF)
    half = second.shape[0] // 2
    upper_ref[...] = second[:half]
    lower_ref[...] = second[half:]


def to_second(place, heads, pieces, outs, vectors):
    part, count = heads[0].shape
    width = outs[0].shape[1]

    def piece_spec(j):
        return pl.BlockSpec((part, count), lambda i, s: (0, j & 1))

    return pl.pallas_call(
        to_second_kernel,
        grid_spec=pltpu.PrefetchScalarGridSpec(
            num_scalar_prefetch=1,
            grid=(1,),
            in_specs=[whole((part, count))] * 4
            + [piece_spec(j) for j in range(4)]
            + [whole(w.shape) for w in outs]
            + [whole(vectors.shape)],
            out_specs=[whole((count, width))] + [whole((count // 2, width))] * 2,
            scratch_shapes=[pltpu.VMEM((width, count), F32)],
        ),
        out_shape=[shape((count, width), F32)] + [shape((count // 2, width), BF)] * 2,
        compiler_params=params(),
        cost_estimate=cost(4),
        name="to_second",
    )(place[None], *heads, *pieces, *outs, vectors)


def feed_kernel(s0, s1, g0, g1, up_ref, down_ref, bias_ref, *outs):
    for k, (second_ref, g_ref) in enumerate(((s0, g0), (s1, g1))):
        act_ref, pre_ref, grad_ref = outs[3 * k : 3 * k + 3]
        pre_act = dot_nn(second_ref[...], up_ref[...]) + bias_ref[...]
        inside = 0.5 * (1.0 + lax.erf(pre_act * (0.5**0.5)))
        density = jnp.exp(-0.5 * pre_act * pre_act) * 0.3989422804014327
        act_ref[...] = (pre_act * inside).astype(BF)
        grad_act = dot_nt(g_ref[...], down_ref[...])
        grad_pre = (grad_act * (inside + pre_act * density)).astype(BF)
        pre_ref[...] = grad_pre
        grad_ref[...] = dot_nt(grad_pre, up_ref[...]).astype(BF)


def feed_pair(seconds, grad_outs, up, down, bias):
    count, width = seconds[0].shape
    units = up.shape[1]
    arrays = (*seconds, *grad_outs, up, down, bias)
    unit, token = shape((count, units), BF), shape((count, width), BF)
    found = pl.pallas_call(
        feed_kernel,
        grid=(1,),
        in_specs=[whole(a.shape) for a in arrays],
        out_specs=[whole(a.shape) for a in (unit, unit, token) * 2],
        out_shape=[unit, unit, token] * 2,
        compiler_params=params(),
        cost_estimate=cost(5),
        name="feed_pair",
    )(*arrays)
    return found[:3], found[3:]


def rows_of(refs):
    return jnp.concatenate([r[...] for r in refs], 0)


def feed_weight_kernel(*refs):
    s_refs, p_refs, a_refs, g_refs = refs[0:8], refs[8:16], refs[16:24], refs[24:32]
    out_ref, sum_ref = refs[32:]
    up = dot_tn(rows_of(s_refs), rows_of(p_refs))
    out_ref[0] = up.astype(BF)
    down = dot_tn(rows_of(a_refs), rows_of(g_refs))
    out_ref[1] = down.astype(BF)
    total = sum(jnp.sum(p[...].astype(F32), 0, keepdims=True) for p in p_refs)
    sum_ref[...] = jnp.broadcast_to(total, sum_ref.shape)


def feed_weights(seconds, grad_pres, activated, grad_outs):
    width, units = seconds[0].shape[1], grad_pres[0].shape[1]
    arrays = (*seconds, *grad_pres, *activated, *grad_outs)
    return pl.pallas_call(
        feed_weight_kernel,
        grid=(1,),
        in_specs=[whole(a.shape) for a in arrays],
        out_specs=[whole((2, width, units)), whole((8, units))],
        out_shape=[shape((2, width, units), BF), shape((8, units), F32)],
        compiler_params=params(),
        cost_estimate=cost(9),
        name="feed_weights",
    )(*arrays)


def to_heads_kernel(resid_ref, a0, a1, b0, b1, c0, c1, g0, g1, *refs):
    o_refs = refs[0:4]
    vec_ref, low_ref, grad_ref, heads_ref, sums_ref = refs[4:]
    resid = resid_ref[...]
    centered = resid - jnp.mean(resid, -1, keepdims=True)
    spread = jnp.mean(centered * centered, -1, keepdims=True)
    scale = lax.rsqrt(spread + norm_eps)
    unit = centered * scale
    grad_second = sum(rows_of(pair).astype(F32) for pair in ((a0, a1), (b0, b1), (c0, c1)))
    e = grad_second * vec_ref[1:2, :]
    first_mean = jnp.mean(e, -1, keepdims=True)
    second_mean = jnp.mean(e * unit, -1, keepdims=True)
    grad_out = rows_of((g0, g1)).astype(F32)
    grad_resid = grad_out + scale * (e - first_mean - unit * second_mean)
    low = grad_resid.astype(BF)
    low_ref[...] = low
    grad_ref[...] = grad_resid.T
    for j in range(4):
        heads_ref[j] = dot_nt(o_refs[j][...], low).astype(BF)
    rows = [grad_second * unit, grad_second, grad_resid, grad_out]
    rows = [jnp.sum(r, 0, keepdims=True) for r in rows]
    blank = jnp.zeros_like(rows[0])

    sums_ref[...] = jnp.concatenate(rows + [blank] * 4, 0)


def to_heads(resid, terms, grad_outs, outs, vectors):
    count, width = resid.shape
    part = outs[0].shape[0]
    token = whole((count, width))
    arrays = (resid, *terms, *grad_outs, *outs, vectors)
    return pl.pallas_call(
        to_heads_kernel,
        grid=(1,),
        in_specs=[whole(a.shape) for a in arrays],
        out_specs=[token, whole((width, count)), whole((4, part, count)), whole((8, width))],
        out_shape=[
            shape((count, width), BF),
            shape((width, count), F32),
            shape((4, part, count), BF),
            shape((8, width), F32),
        ],
        compiler_params=params(),
        cost_estimate=cost(6),
        name="to_heads",
    )(*arrays)


def rest_kernel(near_ref, far_ref, l0, l1, l2, l3, back_ref, f_near, f_far, out_ref):
    columns, half = near_ref.shape
    quarter = half // 2
    total = dot_nn(near_ref[:, :quarter], l0[...]) + dot_nn(near_ref[:, quarter:], l1[...])
    total += dot_nn(far_ref[:, :quarter], l2[...]) + dot_nn(far_ref[:, quarter:], l3[...])
    out_ref[:columns, :] = total.astype(BF)
    total = dot_nt(back_ref[:, :half], f_near[...]) + dot_nt(back_ref[:, half:], f_far[...])
    out_ref[columns:, :] = total.astype(BF)


def rest_weights(near, far, lows, back, firsts):
    width = firsts[0].shape[0]
    arrays = (near, far, *lows, back, *firsts)
    dims = (near.shape[0] + back.shape[0], width)
    return pl.pallas_call(
        rest_kernel,
        grid=(1,),
        in_specs=[whole(a.shape) for a in arrays],
        out_specs=whole(dims),
        out_shape=shape(dims, BF),
        compiler_params=params(),
        cost_estimate=cost(6),
        name="rest_weights",
    )(*arrays)


def back_kernel(back_ref, w_ref, *outs):
    for j, out_ref in enumerate(outs):
        count = out_ref.shape[1]
        rows = back_ref[:, j * count : (j + 1) * count]
        out_ref[...] = dot_nn(w_ref[...], rows).astype(BF)


def first_grads(back, weight):
    count = back.shape[1] // 4
    width = weight.shape[0]
    return pl.pallas_call(
        back_kernel,
        grid=(1,),
        in_specs=[whole(back.shape), whole(weight.shape)],
        out_specs=[whole((width, count))] * 4,
        out_shape=[shape((width, count), BF)] * 4,
        compiler_params=params(),
        cost_estimate=cost(3),
        name="first_grads",
    )(back, weight)


def finish_kernel(
    where_ref, a_ref, b_ref, c_ref, e0, e1, e2, e3, resid_ref, vec_ref,
    cols_ref, rows_ref, sums_ref, emb_ref,
):
    part = e0.shape[0]
    width = 4 * part
    for j, e in enumerate((e0, e1, e2, e3)):
        rows = pl.ds(pl.multiple_of((where_ref[0] ^ j) * part, 64), part)
        emb_ref[rows, :] = e[...].astype(F32)
    grad = a_ref[...].astype(F32) + b_ref[...].astype(F32) + c_ref[...].astype(F32)
    values = emb_ref[...]
    centered = values - jnp.sum(values, 0, keepdims=True) / width
    spread = jnp.sum(centered * centered, 0, keepdims=True) / width
    scale = lax.rsqrt(spread + norm_eps)
    unit = centered * scale
    e = grad * vec_ref[...].T[:, 0:1]
    first_mean = jnp.sum(e, 0, keepdims=True) / width
    second_mean = jnp.sum(e * unit, 0, keepdims=True) / width
    total = resid_ref[...] + scale * (e - first_mean - unit * second_mean)
    emb_ref[...] = total
    for j in range(4):
        rows = pl.ds(pl.multiple_of((where_ref[0] ^ j) * part, 64), part)
        cols_ref[j] = emb_ref[rows, :].astype(BF)
    rows_ref[...] = total.T.astype(BF)
    sums_ref[:, 0:1] = jnp.sum(grad * unit, 1, keepdims=True)
    sums_ref[:, 1:2] = jnp.sum(grad, 1, keepdims=True)


def finish(place, a, b, c, pieces, resid, vectors):
    width, count = a.shape
    part = pieces[0].shape[0]

    def piece_spec(j):
        return pl.BlockSpec((part, count), lambda i, s: (0, j & 1))

    return pl.pallas_call(
        finish_kernel,
        grid_spec=pltpu.PrefetchScalarGridSpec(
            num_scalar_prefetch=1,
            grid=(1,),
            in_specs=[whole(a.shape)] * 3
            + [piece_spec(j) for j in range(4)]
            + [whole(resid.shape), whole(vectors.shape)],
            out_specs=[whole((4, part, count)), whole((count, width)), whole((width, 128))],
            scratch_shapes=[pltpu.VMEM((width, count), F32)],
        ),
        out_shape=[
            shape((4, part, count), BF),
            shape((count, width), BF),
            shape((width, 128), F32),
        ],
        compiler_params=params(),
        cost_estimate=cost(4),
        name="finish",
    )(place[None], a, b, c, *pieces, resid, vectors)


def body(
    gene_ids,
    know_ids,
    lengths,
    tables,
    norm_gain,
    norm_bias,
    qkv_weight,
    qv_bias,
    out_weight,
    out_bias,
    up_weight,
    up_bias,
    down_weight,
    down_bias,
    cotangent,
):
    count = gene_ids.shape[0]
    width = norm_gain.shape[1]
    columns = qkv_weight.shape[2]
    units = up_weight.shape[1]
    head_dim = width // HEADS
    heads_here = columns // head_dim
    owned = tables.shape[0]
    groups = lax.axis_size("dp")
    place = lax.axis_index("tensor")
    group = lax.axis_index("dp")
    quarter = count // 4
    length = lengths[0]
    slots = 128 * (-(-(3 * count // (2 * groups)) // 128))
    know_rows = TABLES * KNOW
    share = know_rows // SHARDS
    start = VOCAB - (groups - 1) * owned
    one_owner = start >= 0 and groups == SHARDS

    def block_at(value, j, size, axis=0):
        return lax.dynamic_slice_in_dim(value, (place ^ j) * size, size, axis)

    def relative(value, size, axis=0):
        return jnp.concatenate([block_at(value, j, size, axis) for j in range(4)], axis)

    ids = relative(gene_ids, quarter)[None]
    codes = relative(know_ids, quarter, 1)
    step = 1
    while step < groups:
        ids = jnp.concatenate([ids, hop(ids, "dp", step)], 0)
        step *= 2
    lists, slot, most = route(group, jnp.int32(0), ids, owned, slots)
    rounds = (most[0, 0] + slots - 1) // slots

    table = tables.T

    picked = pick(lists, table)

    if one_owner:
        held = after(table, ids)[:, start : start + know_rows]
        shards = [held[:, i * share : (i + 1) * share] for i in range(SHARDS)]
        dealt = [lax.ppermute(shards[i], "dp", [(groups - 1, i)]) for i in range(groups - 1)]
        mine = jnp.where(group == groups - 1, shards[-1], jnp.zeros((), BF))
        mine = sum(after(dealt, picked), mine)
        know, order = mine[None], (0,)
        for step in (4, 2, 1):
            know = jnp.concatenate([know, hop(know, "dp", step)], 0)
            order = order + tuple(k | step for k in order)
        turned = group
    else:
        room = jnp.pad(table, ((0, 0), (know_rows, know_rows)))
        begin = jnp.clip(VOCAB - group * owned + know_rows, 0, owned + know_rows)
        know = lax.psum(lax.dynamic_slice_in_dim(room, begin, know_rows, 1), "dp")
        know = jnp.stack([know[:, i * share : (i + 1) * share] for i in range(SHARDS)])
        turned = jnp.int32(0)
        order = tuple(range(SHARDS))

    def exchange(blocks):
        return lax.all_to_all(blocks, "dp", 0, 0, tiled=True)

    def more_rows(carry):
        turn, total = carry
        these, at, _ = route(group, turn, ids, owned, slots)
        return turn + 1, embed_more(at, exchange(pick(these, table)), total)

    blank = jnp.zeros((columns, count), BF)
    _, extra = lax.while_loop(lambda c: c[0] < rounds, more_rows, (jnp.int32(1), blank))

    out_blocks = gather_four(out_weight)
    moved = exchange(picked)
    moved = after(moved, extra, *out_blocks)

    own = [embed(0, turned, order, slot, codes, moved, know, extra)]
    far = [hop(own[0], "tensor", 2)]
    own.append(embed(1, turned, order, slot, codes, after(moved, own[0]), know, extra))
    far.append(hop(after(own[1], far[0]), "tensor", 2))
    near = [hop(o, "tensor", 1) for o in own]
    third = [hop(far[0], "tensor", 1)]

    gain = norm_gain.astype(F32)
    shift = norm_bias.astype(F32)
    weight = qkv_weight.transpose(0, 2, 1).reshape(3 * columns, width)
    weight_down = weight.T
    bias = qv_bias.astype(F32)
    bias = jnp.concatenate([bias[0], jnp.zeros((columns,), F32), bias[1]])[None]
    bias = jnp.pad(bias, ((0, 7), (0, 0)))
    norm_rows = jnp.pad(jnp.stack([gain[0], shift[0]]), ((0, 6), (0, 0)))
    upper = (own[1], near[1], far[0], third[0])
    upper = project(place, upper, norm_rows, weight, bias)
    far[1] = after(far[1], upper)
    third.append(hop(far[1], "tensor", 1))
    lower = (own[0], near[0], far[1], third[1])
    halves = project(place, lower, norm_rows, weight, bias), upper
    pieces = (own[0], near[0], far[1], third[1])
    firsts, projected = zip(*halves)
    spots = relative(jnp.arange(count, dtype=I32), quarter)
    mask = jnp.where(spots < length, 0.0, -1e30).astype(F32)[None]
    valid = jnp.arange(count, dtype=I32) < length
    grad_full = cotangent * valid[:, None].astype(BF)
    eighth = quarter // 2
    grad_outs = []
    for j in range(4):
        rows = block_at(grad_full, j, quarter)
        grad_outs.append((rows[:eighth], rows[eighth:]))
    far_heads, far_lse = attend(*projected, after(mask, grad_outs, weight_down), 1, heads_here, head_dim)
    near_heads, near_lse = attend(*projected, after(mask, far_heads), 0, heads_here, head_dim)

    from_far = [hop(far_heads[:, k * quarter :][:, :quarter], "tensor", 2 + k) for k in (0, 1)]
    near_heads = after(near_heads, from_far)
    heads = [near_heads[:, :quarter], hop(near_heads[:, quarter:], "tensor", 1), *from_far]
    vectors = jnp.stack([out_bias.astype(F32), gain[1], shift[1]])
    up_row = up_bias.astype(F32)[None]

    def feed(rows, grads):
        return feed_pair(rows, grads, up_weight, down_weight, up_row)

    resid, *second = to_second(place, heads, pieces, out_blocks, vectors)
    beside = [hop(s, "tensor", 1) for s in second]
    across = [hop(s, "tensor", 2) for s in second]
    own_blocks = feed(second, grad_outs[0])
    near_blocks = feed(beside, grad_outs[1])
    blocks = [own_blocks, near_blocks]
    seconds, terms = [second, beside], []
    for half in (0, 1):
        rows = after(across[half], blocks)
        rows = [rows, hop(rows, "tensor", 1)]
        found = feed(rows, (grad_outs[2][half], grad_outs[3][half]))
        two = (found[0][2].astype(F32) + hop(found[1][2], "tensor", 1).astype(F32)).astype(BF)
        if half:
            two = after(two, terms[0])
        terms.append(hop(two, "tensor", 2))
        seconds.append(rows)
        blocks.append(found)
    pairs = [grad_outs[0], grad_outs[1]]
    pairs += [(grad_outs[2][k], grad_outs[3][k]) for k in (0, 1)]
    flat = [block for found in blocks for block in found]
    feed_part, unit_sums = feed_weights(
        [rows for pair in seconds for rows in pair],
        [f[1] for f in flat],
        [f[0] for f in flat],
        after([g for pair in pairs for g in pair], two),
    )
    low, grad_resid, grad_heads, sums = to_heads(
        resid,
        after(
            (
                *[f[2] for f in own_blocks],
                *[hop(f[2], "tensor", 1) for f in near_blocks],
                *terms,
            ),
            feed_part,
        ),
        grad_outs[0],
        out_blocks,
        vectors,
    )
    grads = jnp.concatenate(swap_four([grad_heads[j] for j in range(4)]), 1)
    low = after(low, grads)
    lows = swap_four([low] * 4)
    back = attend_back(
        *projected,
        mask,
        (near_heads, far_heads),
        grads,
        (near_lse, far_lse),
        heads_here,
        head_dim,
    )

    def sum_four(parts):
        two = parts[2].astype(F32) + hop(parts[3], "tensor", 1).astype(F32)
        zero = parts[0].astype(F32) + hop(parts[1], "tensor", 1).astype(F32)
        return zero + hop(two.astype(BF), "tensor", 2).astype(F32)

    feed_grad = lax.psum(feed_part, "dp")

    back = after(back, *lows)

    first_grad = first_grads(back, weight_down)

    two = first_grad[2].astype(F32) + hop(first_grad[3], "tensor", 1).astype(F32)
    back_later = after(back, two)
    rest = rest_weights(near_heads, far_heads, lows, back_later, firsts)
    acts = [own_blocks, near_blocks] + [[blocks[2][k], blocks[3][k]] for k in (0, 1)]
    feeds = []
    for pair in acts:
        rows = jnp.concatenate([found[0] for found in pair], 0)
        feeds.append(dot_nn(after(rows, rest), down_weight).astype(BF))
    from_far = hop(two.astype(BF), "tensor", 2)
    from_near = hop(first_grad[1], "tensor", 1)
    by_column, by_row, first_sums = finish(
        place,
        first_grad[0],
        from_near,
        from_far,
        pieces,
        grad_resid,
        norm_rows,
    )
    swapped = swap_four([by_column[j] for j in range(4)])
    near_columns = jnp.concatenate(swapped[:2], 1)
    far_columns = jnp.concatenate(swapped[2:], 1)

    odd_part = know_grads(turned, codes, 0, [near_columns], 2, ())
    far_columns = after(far_columns, odd_part)
    dealt = bucket(slot, near_columns, far_columns, groups, slots)
    sent = exchange(dealt)
    odd_part = know_grads(turned, after(codes, dealt), 1, [far_columns], 2, (odd_part,))
    both = [near_columns, far_columns]
    even_part = know_grads(turned, after(codes, odd_part, feed_grad), 0, both, 0, ())

    def halve(part):
        return part[:2].astype(F32), hop(part[2:], "dp", 1)

    if one_owner:
        odd_own, odd_other = halve(odd_part)
        odd_sum = (odd_own + odd_other.astype(F32)).astype(BF)
        even_own, even_other = halve(even_part)
        rest = lax.psum(rest, "dp", axis_index_groups=[list(range(groups))[::-1]])
        odd_far = hop(after(odd_sum, sent), "dp", 2)
    else:
        rest = lax.psum(after(rest, feed_grad), "dp")
    downs = after(lists, firsts).transpose(0, 2, 1)
    tables_grad = collect(downs, sent, owned)
    if one_owner:
        even_sum = even_own + even_other.astype(F32) + odd_far.astype(F32)
        know_sum = even_sum[0] + hop(even_sum[1].astype(BF), "dp", 4).astype(F32)
        know_sum = after(know_sum.astype(BF), tables_grad)
        last = jnp.where(group == groups - 1, know_sum, jnp.zeros((), BF))
        know_all = [lax.ppermute(know_sum, "dp", [(i, groups - 1)]) for i in range(groups - 1)]
        know_all, order = know_all + [last], tuple(range(SHARDS))
    else:
        know_all = lax.psum(jnp.concatenate([even_part, odd_part], 0), "dp")
        know_sum = know_all
        know_all, order = [know_all[k] for k in range(SHARDS)], (0, 4, 1, 5, 2, 6, 3, 7)

    def more_grads(carry):
        turn, total = carry
        these, at, _ = route(group, turn, ids, owned, slots)
        these = these.transpose(0, 2, 1)
        return turn + 1, collect_more(
            these, exchange(bucket(at, near_columns, far_columns, groups, slots)), total
        )

    _, tables_grad = lax.while_loop(
        lambda c: c[0] < rounds, more_grads, (jnp.int32(1), tables_grad)
    )

    feeds = after(feeds, far_columns)
    out_own = (resid + sum_four(feeds) + down_bias.astype(F32)).astype(BF)

    def spread_rows(own, kind):
        full = jnp.zeros((count, width), kind)
        for j, block in enumerate(gather_four(own)):
            full = lax.dynamic_update_slice_in_dim(
                full, block.astype(kind), (place ^ j) * quarter, 0
            )
        return full

    out = spread_rows(after(out_own, far_columns), BF)
    input_grad = spread_rows(after(by_row, far_columns), F32)

    feed_grad = after(feed_grad, sent).astype(F32)

    qv = jnp.sum(back.reshape(3, columns, count).astype(F32), -1)
    qv = jnp.stack([qv[0], qv[2]])
    qv_wide = lax.dynamic_update_slice_in_dim(
        jnp.zeros((2, width), F32), qv, place * columns, 1
    )
    up_sums = lax.dynamic_update_slice_in_dim(
        jnp.zeros((4, units), F32), unit_sums[0:1], place, 0
    )
    packed = jnp.concatenate(
        [
            first_sums[:, 0],
            first_sums[:, 1],
            sums[0:4].reshape(-1),
            qv_wide.reshape(-1),
            up_sums.reshape(-1),
        ]
    ).reshape(-1, 128)
    packed = after(packed, know_sum)
    for step in (1, 2):
        packed = packed + hop(packed, "tensor", step)
    step = 1
    while step < groups:
        packed = packed + hop(packed, "dp", step)
        step *= 2
    packed = packed.reshape(-1)
    know_all = after(know_all, packed, out, input_grad, feed_grad, rest)
    tables_grad = add_know(VOCAB - group * owned, tables_grad, know_all, order)
    rest = after(rest, tables_grad).astype(F32)
    outw_grad = rest[:columns]
    qkv_grad = rest[columns:].reshape(3, columns, width).transpose(0, 2, 1)
    tops = packed[: 6 * width].reshape(6, width)
    qv_wide = packed[6 * width : 8 * width].reshape(2, width)
    up_sums = packed[8 * width :].reshape(4, units)
    return (
        out,
        input_grad,
        tables_grad.T,
        jnp.stack([tops[0], tops[2]]),
        jnp.stack([tops[1], tops[3]]),
        qkv_grad,
        lax.dynamic_slice_in_dim(qv_wide, place * columns, columns, 1),
        outw_grad,
        tops[4],
        feed_grad[0],
        lax.dynamic_slice_in_dim(up_sums, place, 1, 0)[0],
        feed_grad[1],
        tops[5],
    )


def solution(mesh):
    placed = (
        P("dp"),
        P(None, "dp"),
        P("dp"),
        P("dp", "tensor"),
        P(),
        P(),
        P(None, None, "tensor"),
        P(None, "tensor"),
        P("tensor", None),
        P(),
        P(None, "tensor"),
        P("tensor"),
        P("tensor", None),
        P(),
        P("dp", None),
    )
    return jax.shard_map(
        body,
        mesh=mesh,
        in_specs=placed,
        out_specs=(
            P("dp", None),
            P("dp", None),
            P("dp", "tensor"),
            P(),
            P(),
            P(None, None, "tensor"),
            P(None, "tensor"),
            P("tensor", None),
            P(),
            P(None, "tensor"),
            P("tensor"),
            P("tensor", None),
            P(),
        ),
        check_vma=False,
    )
```

profile of v0, /device:TPU:28, one launch (start us, length us, event | category | flops | bytes accessed | tf_op | source)
XLA Modules:
  0.0 519.3 jit_solution(5404439133388911816)
XLA Ops:
  38.0 11.4 %pick.2 = bf16[8,192,384]{2,1,0:T(8,128)(2,1)} custom-call(s32[8,1,384]{2,1,0:T(1,128)} %get-tuple-element.296.list_ref, bf16[192,5140]{1,0:T(8,128)(2,1)S(1)} %bitcast.108), custom_call_target="tpu_custom_call" | custom-call | flops 10800000000 | bytes 36000000 | tf_op jit(solution)/shard_map/pick/pallas_call | solution.py:162
  56.8 8.3 %collective-permute-done.13 = bf16[1,192,640]{2,1,0:T(8,128)(2,1)S(1)} collective-permute-done((bf16[1,192,640]{2,1,0:T(8,128)(2,1)S(1)}, bf16[1,192,640]{2,1,0:T(8,128)(2,1)S(1)}, u32[]{:S(2)}, u32[]{:S(2)}) %collective-permute-start.13) | collective-permute-done | bytes 245792 | tf_op jit(solution)/shard_map/ppermute | solution.py:70
  65.8 6.6 %all-to-all-start.2 = ((bf16[8,192,384]{2,1,0:T(8,128)(2,1)}), bf16[8,192,384]{2,1,0:T(8,128)(2,1)S(1)}, u32[]{:S(2)}, u32[]{:S(2)}) async-start(bf16[8,192,384]{2,1,0:T(8,128)(2,1)} %pick.2), calls=%async_computation.2 | async-start | bytes 2359296 | tf_op jit(solution)/shard_map/all_to_all | solution.py:969
  74.7 12.7 %collective-permute-done.14 = bf16[2,192,640]{2,1,0:T(8,128)(2,1)S(1)} collective-permute-done((bf16[2,192,640]{2,1,0:T(8,128)(2,1)S(1)}, bf16[2,192,640]{2,1,0:T(8,128)(2,1)S(1)}, u32[]{:S(2)}, u32[]{:S(2)}) %collective-permute-start.14) | collective-permute-done | bytes 491552 | tf_op jit(solution)/shard_map/ppermute | solution.py:70
  92.3 12.2 %collective-permute-done.15 = bf16[4,192,640]{2,1,0:T(8,128)(2,1)S(1)} collective-permute-done((bf16[4,192,640]{2,1,0:T(8,128)(2,1)S(1)}, bf16[4,192,640]{2,1,0:T(8,128)(2,1)S(1)}, u32[]{:S(2)}, u32[]{:S(2)}) %collective-permute-start.15) | collective-permute-done | bytes 983072 | tf_op jit(solution)/shard_map/ppermute | solution.py:70
  107.8 7.1 %embed.2.e0.refs_4_ = bf16[192,1024]{1,0:T(8,128)(2,1)} custom-call(s32[1]{0:T(128)} %bitcast.5.where_ref, s32[1,2048]{1,0:T(1,128)} %get-tuple-element.201.slot_ref, s32[5,2048]{1,0:T(8,128)} %pad_add_fusion.3.code_ref, bf16[8,192,384]{2,1,0:T(8,128)(2,1)} %copy-done.13, bf16[8,192,640]{2,1,0:T(8,128)(2,1)} %pad_maximum_fusion.know_ref, ...), custom_call_target="tpu_custom_call" | custom-call | flops 5400000000 | bytes 18000000 | tf_op jit(solution)/shard_map/embed/pallas_call | solution.py:206
  116.5 6.9 %embed.3.e0 = bf16[192,1024]{1,0:T(8,128)(2,1)} custom-call(s32[1]{0:T(128)} %bitcast.5.where_ref, s32[1,2048]{1,0:T(1,128)} %get-tuple-element.201.slot_ref, s32[5,2048]{1,0:T(8,128)} %pad_add_fusion.3.code_ref, bf16[8,192,384]{2,1,0:T(8,128)(2,1)} %copy-done.13, bf16[8,192,640]{2,1,0:T(8,128)(2,1)} %pad_maximum_fusion.know_ref, ...), custom_call_target="tpu_custom_call" | custom-call | flops 5400000000 | bytes 18000000 | tf_op jit(solution)/shard_map/embed/pallas_call | solution.py:206
  128.2 5.6 %project.2 = (bf16[768,1024]{1,0:T(8,128)(2,1)}, bf16[576,1024]{1,0:T(8,128)(2,1)}) custom-call(s32[1]{0:T(128)} %bitcast.4.where_ref, bf16[192,1024]{1,0:T(8,128)(2,1)} %embed.3.e0, bf16[192,1024]{1,0:T(8,128)(2,1)} %copy-done.72, bf16[192,1024]{1,0:T(8,128)(2,1)} %copy-done.71, bf16[192,1024]{1,0:T(8,128)(2,1)} %copy-done.73, ...), custom_call_target="tpu_custom_call" | custom-call | flops 3600000000 | bytes 12000000 | tf_op jit(solution)/shard_map/project/pallas_call | solution.py:444
  145.3 17.0 %attend.2 = (bf16[192,1024]{1,0:T(8,128)(2,1)}, f32[8,1024]{1,0:T(8,128)}) custom-call(bf16[576,1024]{1,0:T(8,128)(2,1)} %get-tuple-element.217.q_ref.far_ref, bf16[576,1024]{1,0:T(8,128)(2,1)} %get-tuple-element.219.near_ref.q_ref, bf16[576,1024]{1,0:T(8,128)(2,1)} %get-tuple-element.217.q_ref.far_ref, f32[1,2048]{1,0:T(1,128)} %compare_select_fusion.mask_ref), custom_call_target="tpu_custom_call" | custom-call | flops 14400000000 | bytes 48000000 | tf_op jit(solution)/shard_map/attend/pallas_call | solution.py:514
  165.2 17.4 %attend.3 = (bf16[192,1024]{1,0:T(8,128)(2,1)}, f32[8,1024]{1,0:T(8,128)}) custom-call(bf16[576,1024]{1,0:T(8,128)(2,1)} %get-tuple-element.219.near_ref.q_ref, bf16[576,1024]{1,0:T(8,128)(2,1)} %get-tuple-element.219.near_ref.q_ref, bf16[576,1024]{1,0:T(8,128)(2,1)} %get-tuple-element.217.q_ref.far_ref, f32[1,2048]{1,0:T(1,128)} %compare_select_fusion.mask_ref), custom_call_target="tpu_custom_call" | custom-call | flops 14400000000 | bytes 48000000 | tf_op jit(solution)/shard_map/attend/pallas_call | solution.py:514
  226.1 9.6 %collective-permute-done.32.c0 = bf16[256,768]{1,0:T(8,128)(2,1)S(1)} collective-permute-done((bf16[256,768]{1,0:T(8,128)(2,1)S(1)}, bf16[256,768]{1,0:T(8,128)(2,1)S(1)}, u32[]{:S(2)}, u32[]{:S(2)}) %collective-permute-start.32) | collective-permute-done | bytes 393248 | tf_op jit(solution)/shard_map/ppermute | solution.py:70
  236.8 11.0 %feed_weights.1 = (bf16[2,768,768]{2,1,0:T(8,128)(2,1)}, f32[8,768]{1,0:T(8,128)}) custom-call(bf16[256,768]{1,0:T(8,128)(2,1)} %get-tuple-element.226.s0.refs_0_, bf16[256,768]{1,0:T(8,128)(2,1)} %get-tuple-element.227.s1.refs_1_, bf16[256,768]{1,0:T(8,128)(2,1)} %copy-done.58, bf16[256,768]{1,0:T(8,128)(2,1)} %copy-done.60, bf16[256,768]{1,0:T(8,128)(2,1)} %copy-done.59, ...), custom_call_target="tpu_custom_call" | custom-call | flops 8099999744 | bytes 27000000 | tf_op jit(solution)/shard_map/feed_weights/pallas_call | solution.py:730
  249.4 6.6 %to_heads.1 = (bf16[512,768]{1,0:T(8,128)(2,1)}, f32[768,512]{1,0:T(8,128)}, bf16[4,192,512]{2,1,0:T(8,128)(2,1)}, f32[8,768]{1,0:T(8,128)}) custom-call(f32[512,768]{1,0:T(8,128)} %get-tuple-element.225.resid_ref, bf16[256,768]{1,0:T(8,128)(2,1)} %get-tuple-element.264.a0, bf16[256,768]{1,0:T(8,128)(2,1)} %get-tuple-element.265.a1, ...), custom_call_target="tpu_custom_call" | custom-call | flops 5400000000 | bytes 18000000 | tf_op jit(solution)/shard_map/to_heads/pallas_call | solution.py:773
  273.1 38.2 %attend_back.1.back_ref = bf16[576,2048]{1,0:T(8,128)(2,1)} custom-call(bf16[576,1024]{1,0:T(8,128)(2,1)} %get-tuple-element.219.near_ref.q_ref, bf16[576,1024]{1,0:T(8,128)(2,1)} %get-tuple-element.217.q_ref.far_ref, f32[1,2048]{1,0:T(1,128)} %compare_select_fusion.mask_ref, bf16[192,1024]{1,0:T(8,128)(2,1)} %get-tuple-element.224.o_near.near_ref, ...), custom_call_target="tpu_custom_call" | custom-call | flops 34200000512 | bytes 114000000 | tf_op jit(solution)/shard_map/attend_back/pallas_call | solution.py:613
  311.4 6.3 %first_grads.1 = (bf16[768,512]{1,0:T(8,128)(2,1)}, bf16[768,512]{1,0:T(8,128)(2,1)}, bf16[768,512]{1,0:T(8,128)(2,1)}, bf16[768,512]{1,0:T(8,128)(2,1)}) custom-call(bf16[576,2048]{1,0:T(8,128)(2,1)} %attend_back.1.back_ref, bf16[768,576]{1,0:T(8,128)(2,1)} %bitcast.111), custom_call_target="tpu_custom_call" | custom-call | flops 2700000000 | bytes 9000000 | tf_op jit(solution)/shard_map/first_grads/pallas_call | solution.py:826
  318.2 7.5 %rest_weights.1 = bf16[768,768]{1,0:T(8,128)(2,1)} custom-call(bf16[192,1024]{1,0:T(8,128)(2,1)} %get-tuple-element.224.o_near.near_ref, bf16[192,1024]{1,0:T(8,128)(2,1)} %get-tuple-element.221.o_far.far_ref, bf16[512,768]{1,0:T(8,128)(2,1)} %get-tuple-element.272.l0, bf16[512,768]{1,0:T(8,128)(2,1)} %copy-done.49, bf16[512,768]{1,0:T(8,128)(2,1)} %copy-done.50, ...), custom_call_target="tpu_custom_call" | custom-call | flops 5400000000 | bytes 18000000 | tf_op jit(solution)/shard_map/rest_weights/pallas_call | solution.py:804
  336.9 15.1 %collective-permute-done.45.c_ref = bf16[768,512]{1,0:T(8,128)(2,1)S(1)} collective-permute-done((bf16[768,512]{1,0:T(8,128)(2,1)S(1)}, bf16[768,512]{1,0:T(8,128)(2,1)S(1)}, u32[]{:S(2)}, u32[]{:S(2)}) %collective-permute-start.45) | collective-permute-done | bytes 786464 | tf_op jit(solution)/shard_map/ppermute | solution.py:70
  371.2 6.9 %bucket.2 = bf16[8,192,384]{2,1,0:T(8,128)(2,1)} custom-call(s32[1,2048]{1,0:T(1,128)} %get-tuple-element.201.slot_ref, bf16[192,1024]{1,0:T(8,128)(2,1)S(1)} %pad_maximum_fusion.9.refs_0_.near_ref, bf16[192,1024]{1,0:T(8,128)(2,1)S(1)} %pad_maximum_fusion.8.far_ref.refs_0_.refs_1_), custom_call_target="tpu_custom_call" | custom-call | flops 180000000 | bytes 600000 | tf_op jit(solution)/shard_map/bucket/pallas_call | solution.py:268
  378.1 8.0 %all-to-all-start.3 = ((bf16[8,192,384]{2,1,0:T(8,128)(2,1)}), bf16[8,192,384]{2,1,0:T(8,128)(2,1)S(1)}, u32[]{:S(2)}, u32[]{:S(2)}) async-start(bf16[8,192,384]{2,1,0:T(8,128)(2,1)} %bucket.2), calls=%async_computation.3 | async-start | bytes 2359296 | tf_op jit(solution)/shard_map/all_to_all | solution.py:969
  395.6 6.9 %know_grads.5 = bf16[4,192,640]{2,1,0:T(8,128)(2,1)} custom-call(s32[1]{0:T(128)} %bitcast.5.where_ref, s32[5,2048]{1,0:T(8,128)} %pad_add_fusion.3.code_ref, bf16[192,1024]{1,0:T(8,128)(2,1)S(1)} %pad_maximum_fusion.9.refs_0_.near_ref, bf16[192,1024]{1,0:T(8,128)(2,1)S(1)} %pad_maximum_fusion.8.far_ref.refs_0_.refs_1_), custom_call_target="tpu_custom_call" | custom-call | flops 180000000 | bytes 600000 | tf_op jit(solution)/shard_map/know_grads/pallas_call | solution.py:303
  423.5 11.3 %collective-permute-done.51 = bf16[512,768]{1,0:T(8,128)(2,1)} collective-permute-done((bf16[512,768]{1,0:T(8,128)(2,1)}, bf16[512,768]{1,0:T(8,128)(2,1)}, u32[]{:S(2)}, u32[]{:S(2)}) %collective-permute-start.51) | collective-permute-done | bytes 786464 | tf_op jit(solution)/shard_map/ppermute | solution.py:70
  441.7 14.3 %collect.1 = f32[192,5140]{1,0:T(8,128)} custom-call(s32[8,384,1]{2,1,0:T(8,128)} %transpose.30.list_ref, bf16[8,192,384]{2,1,0:T(8,128)(2,1)} %copy-done.12), custom_call_target="tpu_custom_call" | custom-call | flops 13500000256 | bytes 45000000 | tf_op jit(solution)/shard_map/collect/pallas_call | solution.py:334
  476.2 7.3 %collective-permute-done.73 = f32[72,128]{1,0:T(8,128)S(1)} collective-permute-done((f32[72,128]{1,0:T(8,128)S(1)}, f32[72,128]{1,0:T(8,128)S(1)}, u32[]{:S(2)}, u32[]{:S(2)}) %collective-permute-start.73) | collective-permute-done | bytes 36896 | tf_op jit(solution)/shard_map/ppermute | solution.py:70
  502.5 7.6 %add_know.1 = f32[192,5140]{1,0:T(8,128)} custom-call(s32[1]{0:T(128)} %bitcast.30.where_ref, f32[192,5140]{1,0:T(8,128)} %get-tuple-element.297.have_ref, bf16[192,640]{1,0:T(8,128)(2,1)} %copy-done.29, bf16[192,640]{1,0:T(8,128)(2,1)} %copy-done.30, bf16[192,640]{1,0:T(8,128)(2,1)} %copy-done.31, ...), custom_call_target="tpu_custom_call", output_to_operand_aliasing={{}: (1, {})} | custom-call | flops 180000000 | bytes 600000 | tf_op jit(solution)/shard_map/add_know/pallas_call | solution.py:375
  (427 shorter events, 240.9 us)
Async XLA Ops:
  65.2 22.2 %collective-permute-start.14 = (bf16[2,192,640]{2,1,0:T(8,128)(2,1)S(1)}, bf16[2,192,640]{2,1,0:T(8,128)(2,1)S(1)}, u32[]{:S(2)}, u32[]{:S(2)}) collective-permute-start(bf16[2,192,640]{2,1,0:T(8,128)(2,1)S(1)} %pad_maximum_fusion.7), channel_id=1, source_target_pairs={{0,8},{4,12},{8,0},{12,4},{16,24},{20,28},{24,16},{28,20},{1,9},{5... | collective-permute-start | bytes 1474568 | tf_op jit(solution)/shard_map/ppermute | solution.py:70
  65.8 40.9 %all-to-all-start.2 = ((bf16[8,192,384]{2,1,0:T(8,128)(2,1)}), bf16[8,192,384]{2,1,0:T(8,128)(2,1)S(1)}, u32[]{:S(2)}, u32[]{:S(2)}) async-start(bf16[8,192,384]{2,1,0:T(8,128)(2,1)} %pick.2), calls=%async_computation.2 | async-start | bytes 2359296 | tf_op jit(solution)/shard_map/all_to_all | solution.py:969
  72.4 323.2 %all-reduce.5.cloned.1.call-start = ((), (), s32[]{:S(2)}) async-start(), calls=%async_computation.4 | async-start | bytes 4718592 | tf_op jit(solution)/shard_map/psum | solution.py:1085
  72.4 33.6 %collective-permute-start.3 = (bf16[192,768]{1,0:T(8,128)(2,1)}, bf16[192,768]{1,0:T(8,128)(2,1)S(1)}, u32[]{:S(2)}, u32[]{:S(2)}) collective-permute-start(bf16[192,768]{1,0:T(8,128)(2,1)} %refs_0_.1), channel_id=1, source_target_pairs={{0,1},{1,0},{2,3},{3,2},{4,5},{5,4},{6,7},{7,6},{8,9},{9,8},{10,11... | collective-permute-start | bytes 884744 | tf_op jit(solution)/shard_map/ppermute | solution.py:70
  72.4 19.9 %collective-permute-start.4 = (bf16[192,768]{1,0:T(8,128)(2,1)}, bf16[192,768]{1,0:T(8,128)(2,1)S(1)}, u32[]{:S(2)}, u32[]{:S(2)}) collective-permute-start(bf16[192,768]{1,0:T(8,128)(2,1)} %refs_0_.1), channel_id=1, source_target_pairs={{0,2},{1,3},{2,0},{3,1},{4,6},{5,7},{6,4},{7,5},{8,10},{9,11},{10,... | collective-permute-start | bytes 884744 | tf_op jit(solution)/shard_map/ppermute | solution.py:70
  225.4 22.5 %collective-permute-start.27 = (bf16[256,768]{1,0:T(8,128)(2,1)S(1)}, bf16[256,768]{1,0:T(8,128)(2,1)S(1)}, u32[]{:S(2)}, u32[]{:S(2)}) collective-permute-start(bf16[256,768]{1,0:T(8,128)(2,1)S(1)} %copy-done.62), channel_id=1, source_target_pairs={{0,1},{1,0},{2,3},{3,2},{4,5},{5,4},{6,7},{7,6},{8,9},{9,8},{10,11... | collective-permute-start | bytes 1179656 | tf_op jit(solution)/shard_map/ppermute | solution.py:70
  225.6 22.2 %collective-permute-start.28 = (bf16[256,768]{1,0:T(8,128)(2,1)S(1)}, bf16[256,768]{1,0:T(8,128)(2,1)S(1)}, u32[]{:S(2)}, u32[]{:S(2)}) collective-permute-start(bf16[256,768]{1,0:T(8,128)(2,1)S(1)} %copy-done.61), channel_id=1, source_target_pairs={{0,1},{1,0},{2,3},{3,2},{4,5},{5,4},{6,7},{7,6},{8,9},{9,8},{10,11... | collective-permute-start | bytes 1179656 | tf_op jit(solution)/shard_map/ppermute | solution.py:70
  263.6 229.2 %all-reduce.7.cloned.1.call-start = ((), (), s32[]{:S(2)}) async-start(), calls=%async_computation.5 | async-start | bytes 2359296 | tf_op jit(solution)/shard_map/psum | solution.py:1129
  271.3 40.1 %collective-permute-start.40 = (bf16[512,768]{1,0:T(8,128)(2,1)S(1)}, bf16[512,768]{1,0:T(8,128)(2,1)S(1)}, u32[]{:S(2)}, u32[]{:S(2)}) collective-permute-start(bf16[512,768]{1,0:T(8,128)(2,1)S(1)} %copy-done.48), channel_id=1, source_target_pairs={{0,1},{1,0},{2,3},{3,2},{4,5},{5,4},{6,7},{7,6},{8,9},{9,8},{10,11... | collective-permute-start | bytes 2359304 | tf_op jit(solution)/shard_map/ppermute | solution.py:70
  271.4 39.9 %collective-permute-start.41 = (bf16[512,768]{1,0:T(8,128)(2,1)S(1)}, bf16[512,768]{1,0:T(8,128)(2,1)S(1)}, u32[]{:S(2)}, u32[]{:S(2)}) collective-permute-start(bf16[512,768]{1,0:T(8,128)(2,1)S(1)} %copy-done.48), channel_id=1, source_target_pairs={{0,2},{1,3},{2,0},{3,1},{4,6},{5,7},{6,4},{7,5},{8,10},{9,11},{10,... | collective-permute-start | bytes 2359304 | tf_op jit(solution)/shard_map/ppermute | solution.py:70
  272.4 39.0 %collective-permute-start.42 = (bf16[512,768]{1,0:T(8,128)(2,1)S(1)}, bf16[512,768]{1,0:T(8,128)(2,1)S(1)}, u32[]{:S(2)}, u32[]{:S(2)}) collective-permute-start(bf16[512,768]{1,0:T(8,128)(2,1)S(1)} %copy-done.48), channel_id=1, source_target_pairs={{0,3},{1,2},{2,1},{3,0},{4,7},{5,6},{6,5},{7,4},{8,11},{9,10},{10,... | collective-permute-start | bytes 2359304 | tf_op jit(solution)/shard_map/ppermute | solution.py:70
  332.0 19.9 %collective-permute-start.45 = (bf16[768,512]{1,0:T(8,128)(2,1)S(1)}, bf16[768,512]{1,0:T(8,128)(2,1)S(1)}, u32[]{:S(2)}, u32[]{:S(2)}) collective-permute-start(bf16[768,512]{1,0:T(8,128)(2,1)S(1)} %fusion.5), channel_id=1, source_target_pairs={{0,2},{1,3},{2,0},{3,1},{4,6},{5,7},{6,4},{7,5},{8,10},{9,11},{10,... | collective-permute-start | bytes 2359304 | tf_op jit(solution)/shard_map/ppermute | solution.py:70
  378.1 45.4 %all-to-all-start.3 = ((bf16[8,192,384]{2,1,0:T(8,128)(2,1)}), bf16[8,192,384]{2,1,0:T(8,128)(2,1)S(1)}, u32[]{:S(2)}, u32[]{:S(2)}) async-start(bf16[8,192,384]{2,1,0:T(8,128)(2,1)} %bucket.2), calls=%async_computation.3 | async-start | bytes 2359296 | tf_op jit(solution)/shard_map/all_to_all | solution.py:969
  386.5 22.2 %collective-permute-start.50 = (bf16[512,768]{1,0:T(8,128)(2,1)}, bf16[512,768]{1,0:T(8,128)(2,1)}, u32[]{:S(2)}, u32[]{:S(2)}) collective-permute-start(bf16[512,768]{1,0:T(8,128)(2,1)} %convolution_convert_fusion), channel_id=1, source_target_pairs={{0,1},{1,0},{2,3},{3,2},{4,5},{5,4},{6,7},{7,6},{8,9},{9,8},{10,11... | collective-permute-start | bytes 2359304 | tf_op jit(solution)/shard_map/ppermute | solution.py:70
  386.7 31.8 %collective-permute-start.55 = (bf16[512,768]{1,0:T(8,128)(2,1)S(1)}, bf16[512,768]{1,0:T(8,128)(2,1)}, u32[]{:S(2)}, u32[]{:S(2)}) collective-permute-start(bf16[512,768]{1,0:T(8,128)(2,1)S(1)} %copy-done.15), channel_id=1, source_target_pairs={{0,1},{1,0},{2,3},{3,2},{4,5},{5,4},{6,7},{7,6},{8,9},{9,8},{10,11... | collective-permute-start | bytes 2359304 | tf_op jit(solution)/shard_map/ppermute | solution.py:70
  387.3 31.3 %collective-permute-start.56 = (bf16[512,768]{1,0:T(8,128)(2,1)S(1)}, bf16[512,768]{1,0:T(8,128)(2,1)}, u32[]{:S(2)}, u32[]{:S(2)}) collective-permute-start(bf16[512,768]{1,0:T(8,128)(2,1)S(1)} %copy-done.15), channel_id=1, source_target_pairs={{0,2},{1,3},{2,0},{3,1},{4,6},{5,7},{6,4},{7,5},{8,10},{9,11},{10,... | collective-permute-start | bytes 2359304 | tf_op jit(solution)/shard_map/ppermute | solution.py:70
  388.2 35.3 %collective-permute-start.49 = (bf16[512,768]{1,0:T(8,128)(2,1)}, bf16[512,768]{1,0:T(8,128)(2,1)}, u32[]{:S(2)}, u32[]{:S(2)}) collective-permute-start(bf16[512,768]{1,0:T(8,128)(2,1)} %convolution_convert_fusion.2), channel_id=1, source_target_pairs={{0,1},{1,0},{2,3},{3,2},{4,5},{5,4},{6,7},{7,6},{8,9},{9,8},{10,11... | collective-permute-start | bytes 2359304 | tf_op jit(solution)/shard_map/ppermute | solution.py:70
  395.0 20.5 %collective-permute-start.59 = (bf16[2,192,640]{2,1,0:T(8,128)(2,1)}, bf16[2,192,640]{2,1,0:T(8,128)(2,1)}, u32[]{:S(2)}, u32[]{:S(2)}) collective-permute-start(bf16[2,192,640]{2,1,0:T(8,128)(2,1)} %slice.291), channel_id=1, source_target_pairs={{0,4},{4,0},{8,12},{12,8},{16,20},{20,16},{24,28},{28,24},{1,5},{5... | collective-permute-start | bytes 1474568 | tf_op jit(solution)/shard_map/ppermute | solution.py:70
  408.8 31.6 %collective-permute-start.58 = (bf16[2,192,640]{2,1,0:T(8,128)(2,1)}, bf16[2,192,640]{2,1,0:T(8,128)(2,1)}, u32[]{:S(2)}, u32[]{:S(2)}) collective-permute-start(bf16[2,192,640]{2,1,0:T(8,128)(2,1)} %slice.289), channel_id=1, source_target_pairs={{0,4},{4,0},{8,12},{12,8},{16,20},{20,16},{24,28},{28,24},{1,5},{5... | collective-permute-start | bytes 1474568 | tf_op jit(solution)/shard_map/ppermute | solution.py:70
  418.5 19.5 %collective-permute-start.57 = (bf16[512,768]{1,0:T(8,128)(2,1)}, bf16[512,768]{1,0:T(8,128)(2,1)}, u32[]{:S(2)}, u32[]{:S(2)}) collective-permute-start(bf16[512,768]{1,0:T(8,128)(2,1)} %collective-permute-done.56), channel_id=1, source_target_pairs={{0,1},{1,0},{2,3},{3,2},{4,5},{5,4},{6,7},{7,6},{8,9},{9,8},{10,11... | collective-permute-start | bytes 2359304 | tf_op jit(solution)/shard_map/ppermute | solution.py:70
  436.8 29.2 %collective-permute-start.52 = (bf16[512,768]{1,0:T(8,128)(2,1)S(1)}, bf16[512,768]{1,0:T(8,128)(2,1)S(1)}, u32[]{:S(2)}, u32[]{:S(2)}) collective-permute-start(bf16[512,768]{1,0:T(8,128)(2,1)S(1)} %add_convert_fusion), channel_id=1, source_target_pairs={{0,1},{1,0},{2,3},{3,2},{4,5},{5,4},{6,7},{7,6},{8,9},{9,8},{10,11... | collective-permute-start | bytes 2359304 | tf_op jit(solution)/shard_map/ppermute | solution.py:70
  436.9 26.1 %collective-permute-start.53 = (bf16[512,768]{1,0:T(8,128)(2,1)S(1)}, bf16[512,768]{1,0:T(8,128)(2,1)S(1)}, u32[]{:S(2)}, u32[]{:S(2)}) collective-permute-start(bf16[512,768]{1,0:T(8,128)(2,1)S(1)} %add_convert_fusion), channel_id=1, source_target_pairs={{0,2},{1,3},{2,0},{3,1},{4,6},{5,7},{6,4},{7,5},{8,10},{9,11},{10,... | collective-permute-start | bytes 2359304 | tf_op jit(solution)/shard_map/ppermute | solution.py:70
  463.0 25.6 %collective-permute-start.54 = (bf16[512,768]{1,0:T(8,128)(2,1)S(1)}, bf16[512,768]{1,0:T(8,128)(2,1)S(1)}, u32[]{:S(2)}, u32[]{:S(2)}) collective-permute-start(bf16[512,768]{1,0:T(8,128)(2,1)S(1)} %collective-permute-done.53), channel_id=1, source_target_pairs={{0,1},{1,0},{2,3},{3,2},{4,5},{5,4},{6,7},{7,6},{8,9},{9,8},{10,11... | collective-permute-start | bytes 2359304 | tf_op jit(solution)/shard_map/ppermute | solution.py:70
  472.2 20.5 %collective-permute-start.64 = (bf16[192,640]{1,0:T(8,128)(2,1)S(1)}, bf16[192,640]{1,0:T(8,128)(2,1)S(1)}, u32[]{:S(2)}, u32[]{:S(2)}) collective-permute-start(bf16[192,640]{1,0:T(8,128)(2,1)S(1)} %fusion.1), channel_id=1, source_target_pairs={{8,28},{9,29},{10,30},{11,31}} | collective-permute-start | bytes 737288 | tf_op jit(solution)/shard_map/ppermute | solution.py:1140
  (130 other events, 1021.7 us)
Sparse Core Ops, SparseCore 0:
  263.7 108.2 all-reduce.4
  375.9 100.3 all-reduce.6
where the time goes:
time: 527 us; the launch traced here: 519 us
  Pallas kernels  221 us (42%)
  waiting for transfers between devices  120 us (23%)
  starting transfers between devices  67.5 us (13%)
  local copies, waits for them, and re-layouts  52.8 us (10%)
  other arithmetic  32.6 us (6%)
  between operations  16.8 us (3%)
  matrix products  8.12 us (2%)
    ppermute x60, waiting for transfers between devices, hop(): return lax.ppermute(value, axis, [(i, i ^ flip) for i in range(count)])  106 us
    pallas_call x1, Pallas kernels, attend_back(): pl.pallas_call(partial(attend_back_kernel, heads=heads, head_dim=head_dim...  38.2 us
    pallas_call x2, Pallas kernels, attend(): pl.pallas_call(partial(attend_kernel, heads=heads, head_dim=head_dim), gr...  34.3 us
    ppermute x60, starting transfers between devices, hop(): return lax.ppermute(value, axis, [(i, i ^ flip) for i in range(count)])  34.2 us
    pallas_call x4, Pallas kernels, feed_pair(): pl.pallas_call(feed_kernel, grid=(1,), in_specs=[whole(a.shape) for a in...  20 us
    pallas_call x3, Pallas kernels, know_grads(): pl.pallas_call(partial(know_grad_kernel, base=base, parts=len(data)), gri...  16.5 us
    all_to_all x2, starting transfers between devices, exchange(): return lax.all_to_all(blocks, 'dp', 0, 0, tiled=True)  14.6 us
    pallas_call x1, Pallas kernels, collect(): pl.pallas_call(collect_kernel, grid=(pl.cdiv(owned, block),), in_specs=[p...  14.3 us
  transfers between devices with their start and end apart: 78, of which 25 were waited for; matrix products, arithmetic and copies ran while one was open for 14% of the time, Pallas kernels for 33%

commit v1 on v0

--- a/solution.py
+++ b/solution.py
@@ -606,7 +606,7 @@
     rows, half = near.shape
     count = 2 * half
     columns = heads * head_dim
-    block = 256
+    block = min(512, half)
     arrays = (near, far, mask, *out, grad, *lse)
     specs = [whole(a.shape) for a in arrays]
     specs[5] = pl.BlockSpec((columns, block), lambda i: (0, i))

time: 527 us -> 527 us (level)
  transfers between devices with their start and end apart: 78 -> 78, of which waited for: 25 -> 26; matrix products, arithmetic and copies ran while one was open for 14% -> 14% of each run, Pallas kernels for 33% -> 33%
where the time goes in v1:
time: 527 us; the launch traced here: 520 us
  Pallas kernels  219 us (42%)
  waiting for transfers between devices  124 us (24%)
  starting transfers between devices  65.4 us (12%)
  local copies, waits for them, and re-layouts  53.1 us (10%)
  other arithmetic  32.6 us (6%)
  between operations  17.1 us (3%)
  matrix products  8.14 us (2%)
    ppermute x60, waiting for transfers between devices, hop(): return lax.ppermute(value, axis, [(i, i ^ flip) for i in range(count)])  109 us
    pallas_call x1, Pallas kernels, attend_back(): pl.pallas_call(partial(attend_back_kernel, heads=heads, head_dim=head_dim...  36.7 us
    pallas_call x2, Pallas kernels, attend(): pl.pallas_call(partial(attend_kernel, heads=heads, head_dim=head_dim), gr...  34.2 us
    ppermute x60, starting transfers between devices, hop(): return lax.ppermute(value, axis, [(i, i ^ flip) for i in range(count)])  32.2 us
    pallas_call x4, Pallas kernels, feed_pair(): pl.pallas_call(feed_kernel, grid=(1,), in_specs=[whole(a.shape) for a in...  20 us
    pallas_call x3, Pallas kernels, know_grads(): pl.pallas_call(partial(know_grad_kernel, base=base, parts=len(data)), gri...  16.5 us
    all_to_all x2, starting transfers between devices, exchange(): return lax.all_to_all(blocks, 'dp', 0, 0, tiled=True)  14.5 us
    pallas_call x1, Pallas kernels, collect(): pl.pallas_call(collect_kernel, grid=(pl.cdiv(owned, block),), in_specs=[p...  14.3 us
  transfers between devices with their start and end apart: 78, of which 26 were waited for; matrix products, arithmetic and copies ran while one was open for 14% of the time, Pallas kernels for 33%

profile of v1, /device:TPU:28, one launch (start us, length us, event | category | flops | bytes accessed | tf_op | source)
XLA Modules:
  0.0 519.9 jit_solution(9220471125497830786)
XLA Ops:
  38.0 11.4 %pick.2 = bf16[8,192,384]{2,1,0:T(8,128)(2,1)} custom-call(s32[8,1,384]{2,1,0:T(1,128)} %get-tuple-element.296.list_ref, bf16[192,5140]{1,0:T(8,128)(2,1)S(1)} %bitcast.108), custom_call_target="tpu_custom_call" | custom-call | flops 10800000000 | bytes 36000000 | tf_op jit(solution)/shard_map/pick/pallas_call | solution.py:162
  56.8 8.3 %collective-permute-done.13 = bf16[1,192,640]{2,1,0:T(8,128)(2,1)S(1)} collective-permute-done((bf16[1,192,640]{2,1,0:T(8,128)(2,1)S(1)}, bf16[1,192,640]{2,1,0:T(8,128)(2,1)S(1)}, u32[]{:S(2)}, u32[]{:S(2)}) %collective-permute-start.13) | collective-permute-done | bytes 245792 | tf_op jit(solution)/shard_map/ppermute | solution.py:70
  65.8 6.6 %all-to-all-start.2 = ((bf16[8,192,384]{2,1,0:T(8,128)(2,1)}), bf16[8,192,384]{2,1,0:T(8,128)(2,1)S(1)}, u32[]{:S(2)}, u32[]{:S(2)}) async-start(bf16[8,192,384]{2,1,0:T(8,128)(2,1)} %pick.2), calls=%async_computation.2 | async-start | bytes 2359296 | tf_op jit(solution)/shard_map/all_to_all | solution.py:969
  74.7 12.7 %collective-permute-done.14 = bf16[2,192,640]{2,1,0:T(8,128)(2,1)S(1)} collective-permute-done((bf16[2,192,640]{2,1,0:T(8,128)(2,1)S(1)}, bf16[2,192,640]{2,1,0:T(8,128)(2,1)S(1)}, u32[]{:S(2)}, u32[]{:S(2)}) %collective-permute-start.14) | collective-permute-done | bytes 491552 | tf_op jit(solution)/shard_map/ppermute | solution.py:70
  92.3 12.2 %collective-permute-done.15 = bf16[4,192,640]{2,1,0:T(8,128)(2,1)S(1)} collective-permute-done((bf16[4,192,640]{2,1,0:T(8,128)(2,1)S(1)}, bf16[4,192,640]{2,1,0:T(8,128)(2,1)S(1)}, u32[]{:S(2)}, u32[]{:S(2)}) %collective-permute-start.15) | collective-permute-done | bytes 983072 | tf_op jit(solution)/shard_map/ppermute | solution.py:70
  107.8 7.1 %embed.2.e0.refs_4_ = bf16[192,1024]{1,0:T(8,128)(2,1)} custom-call(s32[1]{0:T(128)} %bitcast.5.where_ref, s32[1,2048]{1,0:T(1,128)} %get-tuple-element.201.slot_ref, s32[5,2048]{1,0:T(8,128)} %pad_add_fusion.3.code_ref, bf16[8,192,384]{2,1,0:T(8,128)(2,1)} %copy-done.13, bf16[8,192,640]{2,1,0:T(8,128)(2,1)} %pad_maximum_fusion.know_ref, ...), custom_call_target="tpu_custom_call" | custom-call | flops 5400000000 | bytes 18000000 | tf_op jit(solution)/shard_map/embed/pallas_call | solution.py:206
  116.5 6.9 %embed.3.e0 = bf16[192,1024]{1,0:T(8,128)(2,1)} custom-call(s32[1]{0:T(128)} %bitcast.5.where_ref, s32[1,2048]{1,0:T(1,128)} %get-tuple-element.201.slot_ref, s32[5,2048]{1,0:T(8,128)} %pad_add_fusion.3.code_ref, bf16[8,192,384]{2,1,0:T(8,128)(2,1)} %copy-done.13, bf16[8,192,640]{2,1,0:T(8,128)(2,1)} %pad_maximum_fusion.know_ref, ...), custom_call_target="tpu_custom_call" | custom-call | flops 5400000000 | bytes 18000000 | tf_op jit(solution)/shard_map/embed/pallas_call | solution.py:206
  128.2 5.6 %project.2 = (bf16[768,1024]{1,0:T(8,128)(2,1)}, bf16[576,1024]{1,0:T(8,128)(2,1)}) custom-call(s32[1]{0:T(128)} %bitcast.4.where_ref, bf16[192,1024]{1,0:T(8,128)(2,1)} %embed.3.e0, bf16[192,1024]{1,0:T(8,128)(2,1)} %copy-done.72, bf16[192,1024]{1,0:T(8,128)(2,1)} %copy-done.71, bf16[192,1024]{1,0:T(8,128)(2,1)} %copy-done.73, ...), custom_call_target="tpu_custom_call" | custom-call | flops 3600000000 | bytes 12000000 | tf_op jit(solution)/shard_map/project/pallas_call | solution.py:444
  145.3 17.0 %attend.2 = (bf16[192,1024]{1,0:T(8,128)(2,1)}, f32[8,1024]{1,0:T(8,128)}) custom-call(bf16[576,1024]{1,0:T(8,128)(2,1)} %get-tuple-element.217.q_ref.far_ref, bf16[576,1024]{1,0:T(8,128)(2,1)} %get-tuple-element.219.near_ref.q_ref, bf16[576,1024]{1,0:T(8,128)(2,1)} %get-tuple-element.217.q_ref.far_ref, f32[1,2048]{1,0:T(1,128)} %compare_select_fusion.mask_ref), custom_call_target="tpu_custom_call" | custom-call | flops 14400000000 | bytes 48000000 | tf_op jit(solution)/shard_map/attend/pallas_call | solution.py:514
  165.2 17.2 %attend.3 = (bf16[192,1024]{1,0:T(8,128)(2,1)}, f32[8,1024]{1,0:T(8,128)}) custom-call(bf16[576,1024]{1,0:T(8,128)(2,1)} %get-tuple-element.219.near_ref.q_ref, bf16[576,1024]{1,0:T(8,128)(2,1)} %get-tuple-element.219.near_ref.q_ref, bf16[576,1024]{1,0:T(8,128)(2,1)} %get-tuple-element.217.q_ref.far_ref, f32[1,2048]{1,0:T(1,128)} %compare_select_fusion.mask_ref), custom_call_target="tpu_custom_call" | custom-call | flops 14400000000 | bytes 48000000 | tf_op jit(solution)/shard_map/attend/pallas_call | solution.py:514
  226.2 9.6 %collective-permute-done.32.c0 = bf16[256,768]{1,0:T(8,128)(2,1)S(1)} collective-permute-done((bf16[256,768]{1,0:T(8,128)(2,1)S(1)}, bf16[256,768]{1,0:T(8,128)(2,1)S(1)}, u32[]{:S(2)}, u32[]{:S(2)}) %collective-permute-start.32) | collective-permute-done | bytes 393248 | tf_op jit(solution)/shard_map/ppermute | solution.py:70
  236.8 11.0 %feed_weights.1 = (bf16[2,768,768]{2,1,0:T(8,128)(2,1)}, f32[8,768]{1,0:T(8,128)}) custom-call(bf16[256,768]{1,0:T(8,128)(2,1)} %get-tuple-element.226.s0.refs_0_, bf16[256,768]{1,0:T(8,128)(2,1)} %get-tuple-element.227.s1.refs_1_, bf16[256,768]{1,0:T(8,128)(2,1)} %copy-done.58, bf16[256,768]{1,0:T(8,128)(2,1)} %copy-done.60, bf16[256,768]{1,0:T(8,128)(2,1)} %copy-done.59, ...), custom_call_target="tpu_custom_call" | custom-call | flops 8099999744 | bytes 27000000 | tf_op jit(solution)/shard_map/feed_weights/pallas_call | solution.py:730
  249.5 6.6 %to_heads.1 = (bf16[512,768]{1,0:T(8,128)(2,1)}, f32[768,512]{1,0:T(8,128)}, bf16[4,192,512]{2,1,0:T(8,128)(2,1)}, f32[8,768]{1,0:T(8,128)}) custom-call(f32[512,768]{1,0:T(8,128)} %get-tuple-element.225.resid_ref, bf16[256,768]{1,0:T(8,128)(2,1)} %get-tuple-element.264.a0, bf16[256,768]{1,0:T(8,128)(2,1)} %get-tuple-element.265.a1, ...), custom_call_target="tpu_custom_call" | custom-call | flops 5400000000 | bytes 18000000 | tf_op jit(solution)/shard_map/to_heads/pallas_call | solution.py:773
  273.2 36.7 %attend_back.1.back_ref = bf16[576,2048]{1,0:T(8,128)(2,1)} custom-call(bf16[576,1024]{1,0:T(8,128)(2,1)} %get-tuple-element.219.near_ref.q_ref, bf16[576,1024]{1,0:T(8,128)(2,1)} %get-tuple-element.217.q_ref.far_ref, f32[1,2048]{1,0:T(1,128)} %compare_select_fusion.mask_ref, bf16[192,1024]{1,0:T(8,128)(2,1)} %get-tuple-element.224.o_near.near_ref, ...), custom_call_target="tpu_custom_call" | custom-call | flops 34200000512 | bytes 114000000 | tf_op jit(solution)/shard_map/attend_back/pallas_call | solution.py:613
  309.9 6.3 %first_grads.1 = (bf16[768,512]{1,0:T(8,128)(2,1)}, bf16[768,512]{1,0:T(8,128)(2,1)}, bf16[768,512]{1,0:T(8,128)(2,1)}, bf16[768,512]{1,0:T(8,128)(2,1)}) custom-call(bf16[576,2048]{1,0:T(8,128)(2,1)} %attend_back.1.back_ref, bf16[768,576]{1,0:T(8,128)(2,1)} %bitcast.111), custom_call_target="tpu_custom_call" | custom-call | flops 2700000000 | bytes 9000000 | tf_op jit(solution)/shard_map/first_grads/pallas_call | solution.py:826
  316.8 7.5 %rest_weights.1 = bf16[768,768]{1,0:T(8,128)(2,1)} custom-call(bf16[192,1024]{1,0:T(8,128)(2,1)} %get-tuple-element.224.o_near.near_ref, bf16[192,1024]{1,0:T(8,128)(2,1)} %get-tuple-element.221.o_far.far_ref, bf16[512,768]{1,0:T(8,128)(2,1)} %get-tuple-element.272.l0, bf16[512,768]{1,0:T(8,128)(2,1)} %copy-done.49, bf16[512,768]{1,0:T(8,128)(2,1)} %copy-done.50, ...), custom_call_target="tpu_custom_call" | custom-call | flops 5400000000 | bytes 18000000 | tf_op jit(solution)/shard_map/rest_weights/pallas_call | solution.py:804
  335.4 15.1 %collective-permute-done.45.c_ref = bf16[768,512]{1,0:T(8,128)(2,1)S(1)} collective-permute-done((bf16[768,512]{1,0:T(8,128)(2,1)S(1)}, bf16[768,512]{1,0:T(8,128)(2,1)S(1)}, u32[]{:S(2)}, u32[]{:S(2)}) %collective-permute-start.45) | collective-permute-done | bytes 786464 | tf_op jit(solution)/shard_map/ppermute | solution.py:70
  369.8 6.9 %bucket.2 = bf16[8,192,384]{2,1,0:T(8,128)(2,1)} custom-call(s32[1,2048]{1,0:T(1,128)} %get-tuple-element.201.slot_ref, bf16[192,1024]{1,0:T(8,128)(2,1)S(1)} %pad_maximum_fusion.9.refs_0_.near_ref, bf16[192,1024]{1,0:T(8,128)(2,1)S(1)} %pad_maximum_fusion.8.far_ref.refs_0_.refs_1_), custom_call_target="tpu_custom_call" | custom-call | flops 180000000 | bytes 600000 | tf_op jit(solution)/shard_map/bucket/pallas_call | solution.py:268
  376.7 8.0 %all-to-all-start.3 = ((bf16[8,192,384]{2,1,0:T(8,128)(2,1)}), bf16[8,192,384]{2,1,0:T(8,128)(2,1)S(1)}, u32[]{:S(2)}, u32[]{:S(2)}) async-start(bf16[8,192,384]{2,1,0:T(8,128)(2,1)} %bucket.2), calls=%async_computation.3 | async-start | bytes 2359296 | tf_op jit(solution)/shard_map/all_to_all | solution.py:969
  394.3 6.9 %know_grads.5 = bf16[4,192,640]{2,1,0:T(8,128)(2,1)} custom-call(s32[1]{0:T(128)} %bitcast.5.where_ref, s32[5,2048]{1,0:T(8,128)} %pad_add_fusion.3.code_ref, bf16[192,1024]{1,0:T(8,128)(2,1)S(1)} %pad_maximum_fusion.9.refs_0_.near_ref, bf16[192,1024]{1,0:T(8,128)(2,1)S(1)} %pad_maximum_fusion.8.far_ref.refs_0_.refs_1_), custom_call_target="tpu_custom_call" | custom-call | flops 180000000 | bytes 600000 | tf_op jit(solution)/shard_map/know_grads/pallas_call | solution.py:303
  422.4 10.9 %collective-permute-done.51 = bf16[512,768]{1,0:T(8,128)(2,1)} collective-permute-done((bf16[512,768]{1,0:T(8,128)(2,1)}, bf16[512,768]{1,0:T(8,128)(2,1)}, u32[]{:S(2)}, u32[]{:S(2)}) %collective-permute-start.51) | collective-permute-done | bytes 786464 | tf_op jit(solution)/shard_map/ppermute | solution.py:70
  440.1 14.3 %collect.1 = f32[192,5140]{1,0:T(8,128)} custom-call(s32[8,384,1]{2,1,0:T(8,128)} %transpose.30.list_ref, bf16[8,192,384]{2,1,0:T(8,128)(2,1)} %copy-done.12), custom_call_target="tpu_custom_call" | custom-call | flops 13500000256 | bytes 45000000 | tf_op jit(solution)/shard_map/collect/pallas_call | solution.py:334
  474.3 9.3 %collective-permute-done.73 = f32[72,128]{1,0:T(8,128)S(1)} collective-permute-done((f32[72,128]{1,0:T(8,128)S(1)}, f32[72,128]{1,0:T(8,128)S(1)}, u32[]{:S(2)}, u32[]{:S(2)}) %collective-permute-start.73) | collective-permute-done | bytes 36896 | tf_op jit(solution)/shard_map/ppermute | solution.py:70
  502.8 7.6 %add_know.1 = f32[192,5140]{1,0:T(8,128)} custom-call(s32[1]{0:T(128)} %bitcast.30.where_ref, f32[192,5140]{1,0:T(8,128)} %get-tuple-element.297.have_ref, bf16[192,640]{1,0:T(8,128)(2,1)} %copy-done.29, bf16[192,640]{1,0:T(8,128)(2,1)} %copy-done.30, bf16[192,640]{1,0:T(8,128)(2,1)} %copy-done.31, ...), custom_call_target="tpu_custom_call", output_to_operand_aliasing={{}: (1, {})} | custom-call | flops 180000000 | bytes 600000 | tf_op jit(solution)/shard_map/add_know/pallas_call | solution.py:375
  (427 shorter events, 241.2 us)
Async XLA Ops:
  65.2 22.2 %collective-permute-start.14 = (bf16[2,192,640]{2,1,0:T(8,128)(2,1)S(1)}, bf16[2,192,640]{2,1,0:T(8,128)(2,1)S(1)}, u32[]{:S(2)}, u32[]{:S(2)}) collective-permute-start(bf16[2,192,640]{2,1,0:T(8,128)(2,1)S(1)} %pad_maximum_fusion.7), channel_id=1, source_target_pairs={{0,8},{4,12},{8,0},{12,4},{16,24},{20,28},{24,16},{28,20},{1,9},{5... | collective-permute-start | bytes 1474568 | tf_op jit(solution)/shard_map/ppermute | solution.py:70
  65.8 40.9 %all-to-all-start.2 = ((bf16[8,192,384]{2,1,0:T(8,128)(2,1)}), bf16[8,192,384]{2,1,0:T(8,128)(2,1)S(1)}, u32[]{:S(2)}, u32[]{:S(2)}) async-start(bf16[8,192,384]{2,1,0:T(8,128)(2,1)} %pick.2), calls=%async_computation.2 | async-start | bytes 2359296 | tf_op jit(solution)/shard_map/all_to_all | solution.py:969
  72.4 321.9 %all-reduce.5.cloned.1.call-start = ((), (), s32[]{:S(2)}) async-start(), calls=%async_computation.4 | async-start | bytes 4718592 | tf_op jit(solution)/shard_map/psum | solution.py:1085
  72.4 33.6 %collective-permute-start.3 = (bf16[192,768]{1,0:T(8,128)(2,1)}, bf16[192,768]{1,0:T(8,128)(2,1)S(1)}, u32[]{:S(2)}, u32[]{:S(2)}) collective-permute-start(bf16[192,768]{1,0:T(8,128)(2,1)} %refs_0_.1), channel_id=1, source_target_pairs={{0,1},{1,0},{2,3},{3,2},{4,5},{5,4},{6,7},{7,6},{8,9},{9,8},{10,11... | collective-permute-start | bytes 884744 | tf_op jit(solution)/shard_map/ppermute | solution.py:70
  72.4 19.9 %collective-permute-start.4 = (bf16[192,768]{1,0:T(8,128)(2,1)}, bf16[192,768]{1,0:T(8,128)(2,1)S(1)}, u32[]{:S(2)}, u32[]{:S(2)}) collective-permute-start(bf16[192,768]{1,0:T(8,128)(2,1)} %refs_0_.1), channel_id=1, source_target_pairs={{0,2},{1,3},{2,0},{3,1},{4,6},{5,7},{6,4},{7,5},{8,10},{9,11},{10,... | collective-permute-start | bytes 884744 | tf_op jit(solution)/shard_map/ppermute | solution.py:70
  225.4 22.5 %collective-permute-start.27 = (bf16[256,768]{1,0:T(8,128)(2,1)S(1)}, bf16[256,768]{1,0:T(8,128)(2,1)S(1)}, u32[]{:S(2)}, u32[]{:S(2)}) collective-permute-start(bf16[256,768]{1,0:T(8,128)(2,1)S(1)} %copy-done.62), channel_id=1, source_target_pairs={{0,1},{1,0},{2,3},{3,2},{4,5},{5,4},{6,7},{7,6},{8,9},{9,8},{10,11... | collective-permute-start | bytes 1179656 | tf_op jit(solution)/shard_map/ppermute | solution.py:70
  225.7 22.2 %collective-permute-start.28 = (bf16[256,768]{1,0:T(8,128)(2,1)S(1)}, bf16[256,768]{1,0:T(8,128)(2,1)S(1)}, u32[]{:S(2)}, u32[]{:S(2)}) collective-permute-start(bf16[256,768]{1,0:T(8,128)(2,1)S(1)} %copy-done.61), channel_id=1, source_target_pairs={{0,1},{1,0},{2,3},{3,2},{4,5},{5,4},{6,7},{7,6},{8,9},{9,8},{10,11... | collective-permute-start | bytes 1179656 | tf_op jit(solution)/shard_map/ppermute | solution.py:70
  263.6 229.3 %all-reduce.7.cloned.1.call-start = ((), (), s32[]{:S(2)}) async-start(), calls=%async_computation.5 | async-start | bytes 2359296 | tf_op jit(solution)/shard_map/psum | solution.py:1129
  271.3 38.6 %collective-permute-start.40 = (bf16[512,768]{1,0:T(8,128)(2,1)S(1)}, bf16[512,768]{1,0:T(8,128)(2,1)S(1)}, u32[]{:S(2)}, u32[]{:S(2)}) collective-permute-start(bf16[512,768]{1,0:T(8,128)(2,1)S(1)} %copy-done.48), channel_id=1, source_target_pairs={{0,1},{1,0},{2,3},{3,2},{4,5},{5,4},{6,7},{7,6},{8,9},{9,8},{10,11... | collective-permute-start | bytes 2359304 | tf_op jit(solution)/shard_map/ppermute | solution.py:70
  271.4 38.4 %collective-permute-start.41 = (bf16[512,768]{1,0:T(8,128)(2,1)S(1)}, bf16[512,768]{1,0:T(8,128)(2,1)S(1)}, u32[]{:S(2)}, u32[]{:S(2)}) collective-permute-start(bf16[512,768]{1,0:T(8,128)(2,1)S(1)} %copy-done.48), channel_id=1, source_target_pairs={{0,2},{1,3},{2,0},{3,1},{4,6},{5,7},{6,4},{7,5},{8,10},{9,11},{10,... | collective-permute-start | bytes 2359304 | tf_op jit(solution)/shard_map/ppermute | solution.py:70
  272.5 37.5 %collective-permute-start.42 = (bf16[512,768]{1,0:T(8,128)(2,1)S(1)}, bf16[512,768]{1,0:T(8,128)(2,1)S(1)}, u32[]{:S(2)}, u32[]{:S(2)}) collective-permute-start(bf16[512,768]{1,0:T(8,128)(2,1)S(1)} %copy-done.48), channel_id=1, source_target_pairs={{0,3},{1,2},{2,1},{3,0},{4,7},{5,6},{6,5},{7,4},{8,11},{9,10},{10,... | collective-permute-start | bytes 2359304 | tf_op jit(solution)/shard_map/ppermute | solution.py:70
  330.6 20.0 %collective-permute-start.45 = (bf16[768,512]{1,0:T(8,128)(2,1)S(1)}, bf16[768,512]{1,0:T(8,128)(2,1)S(1)}, u32[]{:S(2)}, u32[]{:S(2)}) collective-permute-start(bf16[768,512]{1,0:T(8,128)(2,1)S(1)} %fusion.5), channel_id=1, source_target_pairs={{0,2},{1,3},{2,0},{3,1},{4,6},{5,7},{6,4},{7,5},{8,10},{9,11},{10,... | collective-permute-start | bytes 2359304 | tf_op jit(solution)/shard_map/ppermute | solution.py:70
  376.7 45.7 %all-to-all-start.3 = ((bf16[8,192,384]{2,1,0:T(8,128)(2,1)}), bf16[8,192,384]{2,1,0:T(8,128)(2,1)S(1)}, u32[]{:S(2)}, u32[]{:S(2)}) async-start(bf16[8,192,384]{2,1,0:T(8,128)(2,1)} %bucket.2), calls=%async_computation.3 | async-start | bytes 2359296 | tf_op jit(solution)/shard_map/all_to_all | solution.py:969
  385.1 22.4 %collective-permute-start.50 = (bf16[512,768]{1,0:T(8,128)(2,1)}, bf16[512,768]{1,0:T(8,128)(2,1)}, u32[]{:S(2)}, u32[]{:S(2)}) collective-permute-start(bf16[512,768]{1,0:T(8,128)(2,1)} %convolution_convert_fusion), channel_id=1, source_target_pairs={{0,1},{1,0},{2,3},{3,2},{4,5},{5,4},{6,7},{7,6},{8,9},{9,8},{10,11... | collective-permute-start | bytes 2359304 | tf_op jit(solution)/shard_map/ppermute | solution.py:70
  385.2 31.6 %collective-permute-start.55 = (bf16[512,768]{1,0:T(8,128)(2,1)S(1)}, bf16[512,768]{1,0:T(8,128)(2,1)}, u32[]{:S(2)}, u32[]{:S(2)}) collective-permute-start(bf16[512,768]{1,0:T(8,128)(2,1)S(1)} %copy-done.15), channel_id=1, source_target_pairs={{0,1},{1,0},{2,3},{3,2},{4,5},{5,4},{6,7},{7,6},{8,9},{9,8},{10,11... | collective-permute-start | bytes 2359304 | tf_op jit(solution)/shard_map/ppermute | solution.py:70
  385.8 31.0 %collective-permute-start.56 = (bf16[512,768]{1,0:T(8,128)(2,1)S(1)}, bf16[512,768]{1,0:T(8,128)(2,1)}, u32[]{:S(2)}, u32[]{:S(2)}) collective-permute-start(bf16[512,768]{1,0:T(8,128)(2,1)S(1)} %copy-done.15), channel_id=1, source_target_pairs={{0,2},{1,3},{2,0},{3,1},{4,6},{5,7},{6,4},{7,5},{8,10},{9,11},{10,... | collective-permute-start | bytes 2359304 | tf_op jit(solution)/shard_map/ppermute | solution.py:70
  386.8 35.5 %collective-permute-start.49 = (bf16[512,768]{1,0:T(8,128)(2,1)}, bf16[512,768]{1,0:T(8,128)(2,1)}, u32[]{:S(2)}, u32[]{:S(2)}) collective-permute-start(bf16[512,768]{1,0:T(8,128)(2,1)} %convolution_convert_fusion.2), channel_id=1, source_target_pairs={{0,1},{1,0},{2,3},{3,2},{4,5},{5,4},{6,7},{7,6},{8,9},{9,8},{10,11... | collective-permute-start | bytes 2359304 | tf_op jit(solution)/shard_map/ppermute | solution.py:70
  393.7 20.3 %collective-permute-start.59 = (bf16[2,192,640]{2,1,0:T(8,128)(2,1)}, bf16[2,192,640]{2,1,0:T(8,128)(2,1)}, u32[]{:S(2)}, u32[]{:S(2)}) collective-permute-start(bf16[2,192,640]{2,1,0:T(8,128)(2,1)} %slice.291), channel_id=1, source_target_pairs={{0,4},{4,0},{8,12},{12,8},{16,20},{20,16},{24,28},{28,24},{1,5},{5... | collective-permute-start | bytes 1474568 | tf_op jit(solution)/shard_map/ppermute | solution.py:70
  407.4 31.3 %collective-permute-start.58 = (bf16[2,192,640]{2,1,0:T(8,128)(2,1)}, bf16[2,192,640]{2,1,0:T(8,128)(2,1)}, u32[]{:S(2)}, u32[]{:S(2)}) collective-permute-start(bf16[2,192,640]{2,1,0:T(8,128)(2,1)} %slice.289), channel_id=1, source_target_pairs={{0,4},{4,0},{8,12},{12,8},{16,20},{20,16},{24,28},{28,24},{1,5},{5... | collective-permute-start | bytes 1474568 | tf_op jit(solution)/shard_map/ppermute | solution.py:70
  416.8 19.5 %collective-permute-start.57 = (bf16[512,768]{1,0:T(8,128)(2,1)}, bf16[512,768]{1,0:T(8,128)(2,1)}, u32[]{:S(2)}, u32[]{:S(2)}) collective-permute-start(bf16[512,768]{1,0:T(8,128)(2,1)} %collective-permute-done.56), channel_id=1, source_target_pairs={{0,1},{1,0},{2,3},{3,2},{4,5},{5,4},{6,7},{7,6},{8,9},{9,8},{10,11... | collective-permute-start | bytes 2359304 | tf_op jit(solution)/shard_map/ppermute | solution.py:70
  435.3 29.1 %collective-permute-start.52 = (bf16[512,768]{1,0:T(8,128)(2,1)S(1)}, bf16[512,768]{1,0:T(8,128)(2,1)S(1)}, u32[]{:S(2)}, u32[]{:S(2)}) collective-permute-start(bf16[512,768]{1,0:T(8,128)(2,1)S(1)} %add_convert_fusion), channel_id=1, source_target_pairs={{0,1},{1,0},{2,3},{3,2},{4,5},{5,4},{6,7},{7,6},{8,9},{9,8},{10,11... | collective-permute-start | bytes 2359304 | tf_op jit(solution)/shard_map/ppermute | solution.py:70
  435.4 26.9 %collective-permute-start.53 = (bf16[512,768]{1,0:T(8,128)(2,1)S(1)}, bf16[512,768]{1,0:T(8,128)(2,1)S(1)}, u32[]{:S(2)}, u32[]{:S(2)}) collective-permute-start(bf16[512,768]{1,0:T(8,128)(2,1)S(1)} %add_convert_fusion), channel_id=1, source_target_pairs={{0,2},{1,3},{2,0},{3,1},{4,6},{5,7},{6,4},{7,5},{8,10},{9,11},{10,... | collective-permute-start | bytes 2359304 | tf_op jit(solution)/shard_map/ppermute | solution.py:70
  462.3 26.4 %collective-permute-start.54 = (bf16[512,768]{1,0:T(8,128)(2,1)S(1)}, bf16[512,768]{1,0:T(8,128)(2,1)S(1)}, u32[]{:S(2)}, u32[]{:S(2)}) collective-permute-start(bf16[512,768]{1,0:T(8,128)(2,1)S(1)} %collective-permute-done.53), channel_id=1, source_target_pairs={{0,1},{1,0},{2,3},{3,2},{4,5},{5,4},{6,7},{7,6},{8,9},{9,8},{10,11... | collective-permute-start | bytes 2359304 | tf_op jit(solution)/shard_map/ppermute | solution.py:70
  471.7 21.2 %collective-permute-start.64 = (bf16[192,640]{1,0:T(8,128)(2,1)S(1)}, bf16[192,640]{1,0:T(8,128)(2,1)S(1)}, u32[]{:S(2)}, u32[]{:S(2)}) collective-permute-start(bf16[192,640]{1,0:T(8,128)(2,1)S(1)} %fusion.1), channel_id=1, source_target_pairs={{8,28},{9,29},{10,30},{11,31}} | collective-permute-start | bytes 737288 | tf_op jit(solution)/shard_map/ppermute | solution.py:1140
  (130 other events, 1026.5 us)
Sparse Core Ops, SparseCore 0:
  263.7 108.2 all-reduce.4
  375.9 107.7 all-reduce.6
